TPU v7x, 256 devices: a whole 4x4x8 slice. The times are simulated.
256 devices in a mesh: lang: 8 (over x, core), dp: 32 (over z, y).
Axes of the slice: x: 4, y: 4, z: 8, core: 2. Of those that a mesh axis runs over, the one named last changes fastest.
Arguments:
- src_emb: bfloat16 [32768, 768], P(('lang', 'dp')), may hold values from -6 to 6
- tgt_emb: bfloat16 [8, 4096, 768], P(None, ('lang', 'dp')), may hold values from -6 to 6
- slot_group: int32 [8], replicated, may hold values from 0 to 7, each once
- counts: int32 [8], replicated, may hold values from 1024 to 4096, as said below
- align: int32 [8, 4096], P('lang'), may hold values from 0 to 4095, each once within a row
- pair_weight: float32 [8], replicated, may hold values from 4 to 40
Outputs:
- grad_src: bfloat16 [32768, 768], P(('lang', 'dp'))
- grad_tgt: bfloat16 [8, 4096, 768], P(None, ('lang', 'dp'))
- pair_loss: float32 [8], P('lang')
Inputs may be any that keep to these rules, and one draw needn't show every extreme that they name: `counts`: at least one pair has all 4096 sentences live. `align`: each row is a permutation.
All inputs are finite; a program needn't handle non-finite values.
Results may differ from a plain program's by a relative error of at most 0.0057.
Values may be sent and summed in bfloat16 or wider, within the bound.
A program may use at most 64 MiB of HBM per device.

v0:
```python
import math

import jax
import jax.numpy as jnp
from jax import lax
from jax.sharding import PartitionSpec as P

MARGIN = 0.3
LOW_FILL = -1e30


def combined_all(value, axis, combine):
    everything = jax.tree.map(lambda part: lax.all_gather(part, axis), value)
    initial = jax.tree.map(lambda part: part[0], everything)

    def lap(k, so_far):
        return combine(so_far, jax.tree.map(lambda part: part[k], everything))

    return lax.fori_loop(1, lax.axis_size(axis), lap, initial)


def target_index(offset, col_count, row_count, per_slot, data_size):
    position = offset + jnp.arange(col_count, dtype=jnp.int32)
    source = position // row_count
    within = position % row_count
    return (within // per_slot * data_size + source) * per_slot + within % per_slot


def tile_scores(
    src_rows, tile_rows, offset, my_align, col_live_global, per_slot, data_size, inv_root
):
    row_count = src_rows.shape[0]
    tgt_index = target_index(offset, tile_rows.shape[0], row_count, per_slot, data_size)
    raw_dot = lax.dot_general(
        src_rows, tile_rows, (((1,), (1,)), ((), ())), preferred_element_type=jnp.float32
    )
    is_pos = tgt_index[None, :] == my_align[:, None]
    scores_f = raw_dot * inv_root - MARGIN * is_pos.astype(jnp.float32)
    col_ok = col_live_global[tgt_index] > 0.5
    return (scores_f, is_pos, col_ok)


def row_update(old_max, scores_f, col_ok):
    masked = jnp.where(col_ok[None, :], scores_f, LOW_FILL)
    new_max = jnp.maximum(old_max, jnp.max(masked, axis=1))
    fresh = jnp.sum(jnp.where(col_ok[None, :], jnp.exp(scores_f - new_max[:, None]), 0.0), axis=1)
    return (new_max, fresh)


def column_stats(scores_f, row_live):
    col_max = jnp.max(jnp.where(row_live[:, None], scores_f, LOW_FILL), axis=0)
    col_sum = jnp.sum(
        jnp.where(row_live[:, None], jnp.exp(scores_f - col_max[None, :]), 0.0), axis=0
    )
    return (col_max, col_sum)


def grad_block(scores_f, is_pos, col_ok, row_lse, col_lse_all, row_live, weight):
    both_live = row_live[:, None] & col_ok[None, :]
    by_row = jnp.where(both_live, jnp.exp(scores_f - row_lse[:, None]), 0.0)
    by_col = jnp.where(both_live, jnp.exp(scores_f - col_lse_all[None, :]), 0.0)
    pos_hit = (is_pos & row_live[:, None]).astype(jnp.float32)
    return (weight * (by_row + by_col - 2.0 * pos_hit)).astype(jnp.bfloat16)


def merge_columns(first_part, second_part):
    top_val = jnp.maximum(first_part[0], second_part[0])
    summed = first_part[1] * jnp.exp(first_part[0] - top_val) + second_part[1] * jnp.exp(
        second_part[0] - top_val
    )
    return (top_val, summed)


def per_device(src_emb, tgt_emb, slot_group, counts, align, pair_weight):
    lang_size = lax.axis_size("lang")
    data_size = lax.axis_size("dp")
    row_count, emb_width = src_emb.shape
    per_slot = tgt_emb.shape[1]
    pair_rows = row_count * data_size
    inv_root = 1.0 / math.sqrt(emb_width)
    group_index = lax.axis_index("lang")
    shard_index = lax.axis_index("dp")
    slot_ids = jnp.arange(lang_size, dtype=jnp.int32)
    slot_of_group = jnp.zeros((lang_size,), jnp.int32).at[slot_group].set(slot_ids)
    ordered = tgt_emb[slot_of_group]
    arrived = lax.all_to_all(ordered, "lang", split_axis=0, concat_axis=1, tiled=True)
    partner = arrived[0]
    live_count = counts[group_index]
    weight = pair_weight[group_index]
    pair_align = align[0]
    all_rows = jnp.arange(pair_rows, dtype=jnp.int32)
    col_live_global = (
        jnp.zeros((pair_rows,), jnp.float32)
        .at[pair_align]
        .set((all_rows < live_count).astype(jnp.float32))
    )
    my_rows = shard_index * row_count + jnp.arange(row_count, dtype=jnp.int32)
    row_live = my_rows < live_count
    my_align = lax.dynamic_slice_in_dim(pair_align, shard_index * row_count, row_count)
    gathered_index = target_index(0, pair_rows, row_count, per_slot, data_size)
    col_live_gathered = col_live_global[gathered_index]
    start_max = jnp.full((row_count,), LOW_FILL, jnp.float32)
    all_targets = lax.all_gather(partner, "dp", axis=0, tiled=True)
    scores_f, is_pos, col_ok = tile_scores(
        src_emb, all_targets, 0, my_align, col_live_global, per_slot, data_size, inv_root
    )
    row_max, row_sum = row_update(start_max, scores_f, col_ok)
    col_max, col_sum = column_stats(scores_f, row_live)
    pos_score = jnp.sum(jnp.where(is_pos, scores_f, 0.0), axis=1)
    merged_max, merged_sum = combined_all((col_max, col_sum), "dp", merge_columns)
    col_lse_all = merged_max + jnp.log(merged_sum + (1.0 - col_live_gathered))
    col_lse_global = jnp.zeros((pair_rows,), jnp.float32).at[gathered_index].set(col_lse_all)
    row_lse = row_max + jnp.log(row_sum + (1.0 - row_live.astype(jnp.float32)))
    terms = jnp.where(row_live, row_lse + col_lse_global[my_align] - 2.0 * pos_score, 0.0)
    loss_total = lax.psum(jnp.sum(terms), "dp")
    pair_loss = (loss_total / live_count.astype(jnp.float32)).reshape(1)
    grad_tile = grad_block(scores_f, is_pos, col_ok, row_lse, col_lse_all, row_live, weight)
    grad_rows = jnp.dot(grad_tile, all_targets, preferred_element_type=jnp.float32)
    own_terms = lax.psum_scatter(
        lax.dot_general(
            grad_tile, src_emb, (((0,), (0,)), ((), ())), preferred_element_type=jnp.float32
        ),
        "dp",
        scatter_dimension=0,
        tiled=True,
    )
    grad_src = (grad_rows * inv_root).astype(jnp.bfloat16)
    grad_local = (own_terms * inv_root).astype(jnp.bfloat16)
    returned = lax.all_to_all(
        grad_local.reshape(1, row_count, emb_width), "lang", split_axis=1, concat_axis=0, tiled=True
    )
    grad_tgt = returned[slot_group]
    return (grad_src, grad_tgt, pair_loss)


def solution(mesh):
    in_specs = (
        P(("lang", "dp"), None),
        P(None, ("lang", "dp"), None),
        P(),
        P(),
        P("lang", None),
        P(),
    )
    out_specs = (P(("lang", "dp"), None), P(None, ("lang", "dp"), None), P("lang"))
    return jax.shard_map(
        per_device, mesh=mesh, in_specs=in_specs, out_specs=out_specs, check_vma=False
    )
```

profile of v0, /device:TPU:2, one launch (start us, length us, event | category | flops | bytes accessed | tf_op | source)
XLA Modules:
  0.0 611.2 jit_solution(6739788015881884098)
XLA Ops:
  7.2 0.7 compare_select_fusion.9
  7.9 0.6 scatter_custom_fusion.1
  8.6 1.5 gather_fusion.1
  10.0 10.7 %all_to_all.21 = bf16[8,16,768]{2,1,0:T(8,128)(2,1)} all-to-all(bf16[8,16,768]{2,1,0:T(8,128)(2,1)S(1)} %gather_fusion.1), channel_id=1, replica_groups=mesh['lang'=8,'dp'=32] {'lang'}, dimensions={0} | all-to-all | bytes 393216 | tf_op jit(solution)/shard_map/all_to_all | solution.py:86
  20.8 1.2 dynamic_slice.32
  22.1 1.3 dynamic_slice.31
  23.4 0.6 fusion.29
  24.1 0.7 compare_select_fusion.3
  24.8 15.5 %scatter_custom_fusion = f32[4096]{0:T(1024)S(1)} fusion(s32[4096]{0:T(1024)S(1)} %bitcast.43, f32[4096]{0:T(1024)S(1)} %fusion.29, f32[]{:T(128)} %constant.134.clone.1), kind=kCustom, calls=%fused_computation.80 | custom fusion | bytes 16388 | tf_op jit(solution)/shard_map/scatter | solution.py:95
  40.4 23.0 %gather_fusion = f32[4096]{0:T(1024)S(1)} fusion(f32[4096]{0:T(1024)S(1)} %scatter_custom_fusion, s32[4096]{0:T(1024)S(1)} %broadcast_clamp_fusion), kind=kCustom, calls=%fused_computation | custom fusion | bytes 49152 | tf_op jit(solution)/shard_map/gather | solution.py:39
  63.5 0.7 add_compare_fusion
  64.1 0.7 fusion.38
  64.8 0.7 fusion.35
  65.5 45.6 %all-gather.4.cloned.1.call-done = bf16[4096,768]{1,0:T(8,128)(2,1)} async-done(((bf16[128,768]{1,0:T(8,128)(2,1)}), bf16[4096,768]{1,0:T(8,128)(2,1)}) %all-gather.4.cloned.1.call-update) | async-done | bytes 6291472 | tf_op jit(solution)/shard_map/all_gather | solution.py:103
  111.1 4.9 select_reduce_fusion.3
  116.0 48.0 %all-gather = f32[131072]{0:T(1024)S(1)} all-gather(f32[4096]{0:T(1024)S(1)} %get-tuple-element.142), channel_id=2, replica_groups=mesh['lang'=8,'dp'=32] {'dp'}, dimensions={0}, use_global_device_ids=true | all-gather | bytes 540672 | tf_op jit(solution)/shard_map/all_gather | solution.py:13
  164.2 4.1 fusion.6
  168.3 47.5 %all-gather.1 = f32[131072]{0:T(1024)S(1)} all-gather(f32[4096]{0:T(1024)S(1)} %get-tuple-element.139), channel_id=3, replica_groups=mesh['lang'=8,'dp'=32] {'dp'}, dimensions={0}, use_global_device_ids=true | all-gather | bytes 540672 | tf_op jit(solution)/shard_map/all_gather | solution.py:13
  215.7 0.9 reshape.345
  216.6 30.5 %while.17 = (s32[]{:T(128)}, f32[4096]{0:T(1024)S(1)}, f32[4096]{0:T(1024)S(1)}, f32[32,4096]{1,0:T(8,128)S(1)}, f32[32,4096]{1,0:T(8,128)}, /*index=5*/s32[]{:T(128)}, s32[]{:T(128)}, s32[]{:T(128)}) while((s32[]{:T(128)}, f32[4096]{0:T(1024)S(1)}, f32[4096]{0:T(1024)S(1)}, f32[32,4096]{1,0:T(8,128)S(1)}, f32[32,4096]{1,0:T(8,128)}, ...), condition=%wide.region_7.8_spmd, body=%wide.region_6.7_spmd.sunk | while | flops 24581 | bytes 163971 | solution.py:19
  216.6 0.9 constant_dynamic-slice_fusion.4
  217.6 0.9 constant_dynamic-slice_fusion.4
  218.6 0.9 constant_dynamic-slice_fusion.4
  219.5 0.9 constant_dynamic-slice_fusion.4
  220.5 0.9 constant_dynamic-slice_fusion.4
  221.5 0.9 constant_dynamic-slice_fusion.4
  222.5 0.9 constant_dynamic-slice_fusion.4
  223.5 0.9 constant_dynamic-slice_fusion.4
  224.5 0.9 constant_dynamic-slice_fusion.4
  225.4 0.9 constant_dynamic-slice_fusion.4
  226.4 0.9 constant_dynamic-slice_fusion.4
  227.4 0.9 constant_dynamic-slice_fusion.4
  228.4 0.9 constant_dynamic-slice_fusion.4
  229.4 0.9 constant_dynamic-slice_fusion.4
  230.4 0.9 constant_dynamic-slice_fusion.4
  231.3 0.9 constant_dynamic-slice_fusion.4
  232.3 0.9 constant_dynamic-slice_fusion.4
  233.3 0.9 constant_dynamic-slice_fusion.4
  234.3 0.9 constant_dynamic-slice_fusion.4
  235.3 0.9 constant_dynamic-slice_fusion.4
  236.3 0.9 constant_dynamic-slice_fusion.4
  237.2 0.9 constant_dynamic-slice_fusion.4
  238.2 0.9 constant_dynamic-slice_fusion.4
  239.2 0.9 constant_dynamic-slice_fusion.4
  240.2 0.9 constant_dynamic-slice_fusion.4
  241.2 0.9 constant_dynamic-slice_fusion.4
  242.2 0.9 constant_dynamic-slice_fusion.4
  243.1 0.9 constant_dynamic-slice_fusion.4
  244.1 0.9 constant_dynamic-slice_fusion.4
  245.1 0.9 constant_dynamic-slice_fusion.4
  246.1 0.9 constant_dynamic-slice_fusion.4
  247.1 15.5 %scatter_custom_fusion.2 = f32[4096]{0:T(1024)S(1)} fusion(s32[4096]{0:T(1024)S(1)} %bitcast.42, f32[4096]{0:T(1024)S(1)} %log_add_fusion, f32[]{:T(128)} %constant.134.clone.1), kind=kCustom, calls=%fused_computation.78 | custom fusion | bytes 16388 | tf_op jit(solution)/shard_map/scatter | solution.py:112
  262.6 1.1 gather_fusion.3
  263.8 1.3 select_reduce_fusion.4
  265.1 9.0 %fusion.39 = f32[4096,768]{1,0:T(8,128)} fusion(bf16[128,768]{1,0:T(8,128)(2,1)S(1)} %copy-done, f32[128,4096]{0,1:T(8,128)S(1)} %get-tuple-element.159, f32[4096]{0:T(1024)S(1)} %log_add_fusion, f32[128]{0:T(128)S(1)} %get-tuple-element.156, s32[128]{0:T(128)S(1)} %fusion.38, f32[]{:T(128)} %bitcast.2, s32[4096]{0:T(1024)S(1)} %fusion.19, ...), kind=kOutput, calls=%fused_computation.97 | convolution fusion | flops 811597824 | bytes 14914692 | tf_op jit(solution)/shard_map/dot_general | solution.py:120
  274.8 234.3 %reduce-scatter.2.cloned.1.call-done = f32[128,768]{1,0:T(8,128)} async-done(((f32[4096,768]{1,0:T(8,128)}), f32[128,768]{1,0:T(8,128)}) %reduce-scatter.2.cloned.1.call-update) | async-done | bytes 393232 | tf_op jit(solution)/shard_map/reduce_scatter | solution.py:119
  509.1 1.0 fusion.8
  510.4 0.5 broadcast.420
  510.9 1.8 reduce
  512.7 0.7 reshape.359
  513.5 5.0 all-to-all-start.1
  518.4 10.0 %fusion.7 = bf16[128,768]{1,0:T(8,128)(2,1)} fusion(bf16[4096,768]{1,0:T(8,128)(2,1)} %all-gather.4.cloned.1.call-done, f32[128,4096]{0,1:T(8,128)S(1)} %get-tuple-element.159, f32[4096]{0:T(1024)S(1)} %log_add_fusion, f32[128]{0:T(128)S(1)} %get-tuple-element.156, s32[128]{0:T(128)S(1)} %fusion.38, f32[]{:T(128)} %bitcast.2, s32[4096]{0:T(1024)S(1)} %fusion.19, ...), kind=kOutput, calls=%fused_computation.28 | convolution fusion | flops 811794432 | bytes 8623236 | tf_op jit(solution)/shard_map/dot_general | solution.py:118
  528.4 72.7 %psum.7 = f32[]{:T(128)} all-reduce(f32[]{:T(128)} %get-tuple-element.155), channel_id=1, replica_groups=mesh['lang'=8,'dp'=32] {'dp'}, use_global_device_ids=true, to_apply=%region_12.13 | all-reduce | flops 1 | bytes 8 | tf_op jit(solution)/shard_map/psum | solution.py:115
  602.0 1.2 gather_fusion.2
  (55 shorter events, 1.6 us)
Async XLA Ops:
  7.2 103.9 %copy-start = (bf16[128,768]{1,0:T(8,128)(2,1)S(1)}, bf16[128,768]{1,0:T(8,128)(2,1)}, u32[]{:S(2)}) copy-start(bf16[128,768]{1,0:T(8,128)(2,1)} %param.8) | copy-start | bytes 589828
  7.2 103.9 %all-gather.4.cloned.1.call-start = ((), (), s32[]{:S(2)}) async-start(), calls=%async_computation.3 | async-start | bytes 6488064 | tf_op jit(solution)/shard_map/all_gather | solution.py:103
  20.8 488.3 %reduce-scatter.2.cloned.1.call-start = ((), (), s32[]{:S(2)}) async-start(), calls=%async_computation.4 | async-start | bytes 12976128 | tf_op jit(solution)/shard_map/reduce_scatter | solution.py:119
  513.5 88.3 %all-to-all-start.1 = ((bf16[8,2,6144]{2,1,0:T(2,128)(2,1)}), bf16[8,2,6144]{2,1,0:T(2,128)(2,1)S(1)}, u32[]{:S(2)}, u32[]{:S(2)}) async-start(bf16[8,2,6144]{2,1,0:T(2,128)(2,1)} %reshape.359), calls=%async_computation.2 | async-start | bytes 393216 | tf_op jit(solution)/shard_map/all_to_all | solution.py:129
Sparse Core Ops, SparseCore 0:
  20.9 90.1 all-gather.3
  274.2 234.7 reduce-scatter.1
where the time goes:
time: 612 us; the launch traced here: 611 us
  waiting for transfers between devices  280 us (46%)
  blocking collectives  179 us (29%)
  local copies, waits for them, and re-layouts  93.5 us (15%)
  matrix products  23.9 us (4%)
  between operations  16.7 us (3%)
  other arithmetic  12.5 us (2%)
    reduce_scatter x1, waiting for transfers between devices, per_device(): lax.psum_scatter(lax.dot_general(grad_tile, src_emb, (((0,), (0,)), ((),...  234 us
    all_gather x2, blocking collectives, combined_all(): everything = jax.tree.map(lambda part: lax.all_gather(part, axis), value)  95.5 us
    psum x1, blocking collectives, per_device(): loss_total = lax.psum(jnp.sum(terms), 'dp')  72.7 us
    all_gather x1, waiting for transfers between devices, per_device(): all_targets = lax.all_gather(partner, 'dp', axis=0, tiled=True)  45.6 us
    dynamic_slice x31, local copies, waits for them, and re-layouts, lap(): return combine(so_far, jax.tree.map(lambda part: part[k], everything))  29 us
    gather x1, local copies, waits for them, and re-layouts, tile_scores(): col_ok = col_live_global[tgt_index] > 0.5  23 us
    scatter x1, local copies, waits for them, and re-layouts, per_device(): jnp.zeros((pair_rows,), jnp.float32).at[gathered_index].set(col_lse_all)  15.5 us
    scatter x1, local copies, waits for them, and re-layouts, per_device(): col_live_global = jnp.zeros((pair_rows,), jnp.float32).at[pair_align].set...  15.5 us
  transfers between devices with their start and end apart: 3, of which 2 were waited for; matrix products, arithmetic and copies ran while one was open for 9% of the time, Pallas kernels for 0%

commit v1 on v0

v1 whole, which is shorter than its diff:
```python
import functools
import math

import jax
import jax.numpy as jnp
from jax import lax
from jax.experimental import pallas as pl
from jax.experimental.pallas import tpu as pltpu
from jax.sharding import PartitionSpec as P

MARGIN = 0.3
LOW = -1e30
NY = 4
F32 = jnp.float32
BF16 = jnp.bfloat16


def kernel(
    slots, counts, weights, align, x, t, gsrc, gtgt, loss,
    xs, ys, staged, acol, colok, er, ec, rmax, cmax, gm, psrc, ptgt,
    rst_out, rst_in, cst_out, cst_in, lz_out, lz_in, ly_out, ly_in,
    fz_out, fz_in, fy_out, fy_in, back, ret,
    sa, ra, sgz, rgz, sgy, rgy, srs, rrs, scs, rcs, slz, rlz, sly, rly,
    sfz, rfz, sfy, rfy, sb, rb,
):
    nl, per = t.shape[0], t.shape[1]
    nz = xs.shape[0]
    rows, width = x.shape
    half = rows // 2
    inv_root = 1.0 / math.sqrt(width)
    lang, dp = lax.axis_index("lang"), lax.axis_index("dp")
    z, y = dp // NY, dp % NY
    live = counts[lang]
    weight = weights[lang]

    def z_at(k):
        return {"dp": lax.rem(z + k + nz, nz) * NY + y}

    def y_at(k):
        return {"dp": z * NY + lax.rem(y + k + NY, NY)}

    def lang_at(k):
        return {"lang": lax.rem(lang + k + nl, nl)}

    def remote(src, dst, send, recv, to):
        return pltpu.make_async_remote_copy(
            src_ref=src, dst_ref=dst, send_sem=send, recv_sem=recv,
            device_id=to, device_id_type=pl.DeviceIdType.MESH,
        )

    started = []

    def start(copy):
        copy.start()
        started.append(copy)
        return copy

    barrier = pltpu.get_barrier_semaphore()
    peers = [z_at(k) for k in range(1, nz)] + [y_at(k) for k in range(1, NY)]
    peers += [lang_at(k) for k in range(1, nl)]
    for to in peers:
        pl.semaphore_signal(barrier, inc=1, device_id=to, device_id_type=pl.DeviceIdType.MESH)
    xs[0] = x[...]
    for o in range(nl):
        group = lax.rem(lang + o, nl)
        slot = jnp.int32(0)
        for s in range(nl):
            slot = jnp.where(slots[s] == group, s, slot)
        staged[o] = t[slot]
    ys[0, 0:per] = staged[0]
    pl.semaphore_wait(barrier, len(peers))

    def gather_copies(buf, n, send, recv, at):
        copies = {}
        for k in range(n // 2):
            for h in (0, 1):
                part = pl.ds(h * half, half)
                if k < n // 2 - 1 or h == 0:
                    copies[0, k, h] = remote(
                        buf.at[k, part], buf.at[k + 1, part], send.at[0, k, h], recv.at[k + 1, h], at(1)
                    )
                if k < n // 2 - 1 or h == 1:
                    copies[1, k, h] = remote(
                        buf.at[(n - k) % n, part], buf.at[n - 1 - k, part],
                        send.at[1, k, h], recv.at[n - 1 - k, h], at(-1),
                    )
        return copies

    gz = gather_copies(xs, nz, sgz, rgz, z_at)
    gy = gather_copies(ys, NY, sgy, rgy, y_at)
    for h in (0, 1):
        start(gz[0, 0, h])
        start(gz[1, 0, 1 - h])
    spread = [
        start(remote(staged.at[o], ys.at[0, pl.ds(o * per, per)], sa.at[o], ra.at[o], lang_at(o)))
        for o in range(1, nl)
    ]

    lane = lax.broadcasted_iota(jnp.int32, (1, rows), 1)
    sub = lax.broadcasted_iota(jnp.int32, (rows, rows), 0)

    def target_of(q, position):
        source = lax.rem(lang - position // per + nl, nl)
        return (source * (nz * NY) + z * NY + lax.rem(y - q + NY, NY)) * per + position % per

    def first_row(r):
        return (lax.rem(z - r + nz, nz) * NY + y) * rows

    def prepare():
        for q in range(NY):
            mine = target_of(q, sub)

            def seen(ch, so_far, mine=mine):
                at = pl.multiple_of(ch * rows, rows)
                own = align[0:1, pl.ds(at, rows)]
                own = jnp.where(lane + at < live, own, -1)
                return jnp.where(mine == own, 1.0, so_far)

            hit = lax.fori_loop(0, nz * NY, seen, jnp.zeros((rows, rows), F32))
            hit = jnp.broadcast_to(jnp.max(hit, axis=1, keepdims=True), (rows, rows))
            colok[q : q + 1] = hit.T[0:1]
        for r in range(nz):
            own = align[0:1, pl.ds(pl.multiple_of(first_row(r), rows), rows)]
            acol[r] = jnp.broadcast_to(own.astype(F32), (rows, rows)).T

    prepare()

    target_row = jnp.concatenate([target_of(q, lane) for q in range(NY)], axis=1).astype(F32)
    row_in = lax.broadcasted_iota(jnp.int32, (rows, 1), 0)

    def masks(r):
        column = acol[r][:, 0:1]
        pos = column == target_row
        row_ok = row_in + first_row(r) < live
        return pos, row_ok

    def all_targets():
        return ys[...].reshape(NY * rows, width)

    total_pos = [jnp.zeros((1, NY * rows), F32)]

    def scores(r):
        raw = lax.dot_general(
            xs[r], all_targets(), (((1,), (1,)), ((), ())), preferred_element_type=F32
        )
        pos, row_ok = masks(r)
        col_ok = jnp.concatenate([colok[q : q + 1] for q in range(NY)], axis=1) > 0.5
        s = raw * inv_root - jnp.where(pos, MARGIN, 0.0)
        total_pos[0] += jnp.sum(jnp.where(pos & row_ok, s, 0.0), axis=0, keepdims=True)
        s = jnp.where(row_ok & col_ok, s, LOW)
        top = jnp.max(s, axis=1, keepdims=True)
        e = jnp.exp(s - top)
        er[r] = e
        row_lse = top + jnp.log(jnp.sum(e, axis=1, keepdims=True))
        rmax[r] = jnp.broadcast_to(top, (rows, rows))
        rst_out[r : r + 1] = jnp.broadcast_to(row_lse, (rows, rows)).T[0:1]
        top = jnp.max(s, axis=0, keepdims=True)
        e = jnp.exp(s - top)
        ec[r] = e
        cmax[r, 0:1] = top
        cmax[r, 1:2] = top + jnp.log(jnp.sum(e, axis=0, keepdims=True))

    def z_step(k, h):
        for d in (0, 1):
            part = h if d == 0 else 1 - h
            if (d, k, part) in gz:
                gz[d, k, part].wait_recv()
                if (d, k + 1, part) in gz:
                    start(gz[d, k + 1, part])

    z_step(0, 0)
    for o in range(1, nl):
        spread[o - 1].wait_recv()
        if o == nl // 2 - 1:
            start(gy[0, 0, 0])
            start(gy[1, 0, 0])
        if o == nl - 1:
            start(gy[0, 0, 1])
            start(gy[1, 0, 1])
    z_step(0, 1)
    gy[0, 0, 0].wait_recv()
    gy[1, 0, 0].wait_recv()
    start(gy[0, 1, 0])
    z_step(1, 0)
    gy[0, 0, 1].wait_recv()
    gy[1, 0, 1].wait_recv()
    start(gy[1, 1, 1])
    z_step(1, 1)
    gy[0, 1, 0].wait_recv()
    gy[1, 1, 1].wait_recv()
    scores(0)
    for k in range(2, nz // 2):
        for r in (k - 1, nz - k + 1):
            scores(r)
        z_step(k, 0)
        z_step(k, 1)
    for r in (nz // 2 - 1, nz // 2 + 1):
        scores(r)
    scores(nz // 2)

    parts = cmax[:, 1, :]
    top = jnp.max(parts, axis=0, keepdims=True)
    col_part = top + jnp.log(jnp.sum(jnp.exp(parts - top), axis=0, keepdims=True))
    for q in range(NY):
        cst_out[q : q + 1] = col_part[:, q * rows : (q + 1) * rows]
        cst_out[q + NY : q + NY + 1] = col_part[:, q * rows : (q + 1) * rows]
    rst = [start(remote(rst_out, rst_in.at[k], srs.at[k], rrs.at[k], z_at(k))) for k in range(1, nz)]
    cst = [start(remote(cst_out, cst_in.at[k], scs.at[k], rcs.at[k], y_at(k))) for k in range(1, NY)]

    def combine(pieces):
        top = functools.reduce(jnp.maximum, pieces)
        return top + jnp.log(functools.reduce(jnp.add, [jnp.exp(p - top) for p in pieces]))

    def turn(piece, k):
        return jnp.concatenate([piece[piece.shape[0] - k :], piece[: piece.shape[0] - k]], axis=0)

    for copy in cst:
        copy.wait_recv()
    col_lse = combine([cst_out[0:NY]] + [turn(cst_in[k, 0:NY], k) for k in range(1, NY)])
    for copy in rst:
        copy.wait_recv()
    row_lse = combine([rst_out[...]] + [turn(rst_in[k], k) for k in range(1, nz)])

    def gradient(r):
        pos, row_ok = masks(r)
        own = jnp.broadcast_to(row_lse[r : r + 1], (rows, rows)).T
        by_row = jnp.where(row_ok, weight * jnp.exp(rmax[r] - own), 0.0)
        for q in range(NY):
            at = slice(q * rows, (q + 1) * rows)
            by_col = jnp.where(
                colok[q : q + 1] > 0.5, weight * jnp.exp(cmax[r, 0:1, at] - col_lse[q : q + 1]), 0.0
            )
            g = er[r, :, at] * by_row + ec[r, :, at] * by_col
            g = g - jnp.where(pos[:, at] & row_ok, 2.0 * weight, 0.0)
            gm[r, :, at] = g.astype(BF16)

    def source_part(r):
        psrc[r] = jnp.dot(gm[r], all_targets(), preferred_element_type=F32)

    def target_part(q):
        ptgt[q] = lax.dot_general(
            gm[:, :, q * rows : (q + 1) * rows].reshape(nz * rows, rows),
            xs[...].reshape(nz * rows, width),
            (((0,), (0,)), ((), ())),
            preferred_element_type=F32,
        )

    def ring(part, n, out, inn, send, recv, at):
        last = n // 2
        copies = {}

        def slot(d, k):
            return (n - (last + 1 - k)) % n if d == 0 else last + 1 - k

        def step(d, k, h):
            begins = 1 if h == d else 2
            value = part[slot(d, k), h * half : (h + 1) * half]
            if k > begins:
                copies[d, k - 1, h].wait_recv()
                value = value + inn[d, k - 1, h].astype(F32)
            out[d, k, h] = value.astype(BF16)
            copies[d, k, h] = start(
                remote(out.at[d, k, h], inn.at[d, k, h], send.at[d, k, h], recv.at[d, k, h], at(1 if d == 0 else -1))
            )

        def owned(h):
            copies[0, last, h].wait_recv()
            copies[1, last, h].wait_recv()
            value = part[0, h * half : (h + 1) * half]
            value = value + inn[0, last, h].astype(F32) + inn[1, last, h].astype(F32)
            return (value * inv_root).astype(BF16)

        return step, owned

    z_send, z_owned = ring(psrc, nz, fz_out, fz_in, sfz, rfz, z_at)
    y_send, y_owned = ring(ptgt, NY, fy_out, fy_in, sfy, rfy, y_at)
    mid = nz // 2
    gradient(mid)
    source_part(mid)
    z_send(0, 1, 0)
    z_send(1, 1, 1)
    for r in (mid + 1, mid - 1):
        gradient(r)
        source_part(r)
    z_send(0, 2, 1)
    z_send(1, 2, 0)
    for r in range(nz):
        if abs(r - mid) > 1:
            gradient(r)
    target_part(NY // 2)
    y_send(0, 1, 0)
    y_send(1, 1, 1)
    z_send(0, 2, 0)
    z_send(1, 2, 1)
    for q in (1, 3):
        target_part(q)
    y_send(0, 2, 1)
    y_send(1, 2, 0)
    for r in (mid + 2, mid - 2):
        source_part(r)
    z_send(0, 3, 1)
    z_send(1, 3, 0)
    y_send(0, 2, 0)
    y_send(1, 2, 1)
    target_part(0)

    own_rows = jnp.where(lane + first_row(0) < live, row_lse[0:1], 0.0)
    own_cols = jnp.where(colok[0:1] > 0.5, col_lse[0:1], 0.0)
    pos_sum = functools.reduce(jnp.add, [total_pos[0][:, q * rows : (q + 1) * rows] for q in range(NY)])
    lz_out[...] = jnp.broadcast_to(own_rows + own_cols - 2.0 * pos_sum, lz_out.shape)
    lz = [start(remote(lz_out, lz_in.at[k], slz.at[k], rlz.at[k], z_at(k))) for k in range(1, nz)]
    for r in (mid + 3, mid - 3):
        source_part(r % nz)
    source_part(0)
    z_send(0, 3, 0)
    z_send(1, 3, 1)
    for copy in lz:
        copy.wait_recv()
    ly_out[...] = functools.reduce(jnp.add, [lz_out[...]] + [lz_in[k] for k in range(1, nz)])
    ly = [start(remote(ly_out, ly_in.at[k], sly.at[k], rly.at[k], y_at(k))) for k in range(1, NY)]
    z_send(0, 4, 1)
    z_send(1, 4, 0)

    backs = []
    for h in (0, 1):
        value = y_owned(h)
        for i in range(nl // 2):
            o = h * (nl // 2) + i
            if o == 0:
                ret[0] = value[0:per]
            else:
                back[o] = value[i * per : (i + 1) * per]
                backs.append(start(remote(back.at[o], ret.at[o], sb.at[o], rb.at[o], lang_at(-o))))
    z_send(0, 4, 0)
    z_send(1, 4, 1)
    for copy in ly:
        copy.wait_recv()
    everything = functools.reduce(jnp.add, [ly_out[...]] + [ly_in[k] for k in range(1, NY)])
    loss[0] = jnp.sum(everything[0:1]) / live.astype(F32)
    for copy in backs:
        copy.wait_recv()
    for s in range(nl):
        gtgt[s] = ret[lax.rem(slots[s] - lang + nl, nl)]
    for h in (1, 0):
        gsrc[h * half : (h + 1) * half] = z_owned(h)
    for copy in started:
        copy.wait_send()


def per_device(src_emb, tgt_emb, slot_group, counts, align, pair_weight):
    rows, width = src_emb.shape
    nl, per = tgt_emb.shape[0], tgt_emb.shape[1]
    nd = lax.axis_size("dp")
    nz = nd // NY
    cols = NY * rows
    half = rows // 2
    kz, ky = nz // 2 + 1, NY // 2 + 1
    vmem, smem, dma = pltpu.VMEM, pltpu.SMEM, pltpu.SemaphoreType.DMA
    in_vmem, in_smem = pl.BlockSpec(memory_space=vmem), pl.BlockSpec(memory_space=smem)
    scratch = [
        vmem((nz, rows, width), BF16), vmem((NY, rows, width), BF16), vmem((nl, per, width), BF16),
        vmem((nz, rows, rows), F32), vmem((8, rows), F32),
        vmem((nz, rows, cols), F32), vmem((nz, rows, cols), F32),
        vmem((nz, rows, rows), F32), vmem((nz, 8, cols), F32),
        vmem((nz, rows, cols), BF16), vmem((nz, rows, width), F32), vmem((NY, rows, width), F32),
        vmem((nz, rows), F32), vmem((nz, nz, rows), F32), vmem((8, rows), F32), vmem((NY, 8, rows), F32),
        vmem((8, rows), F32), vmem((nz, 8, rows), F32), vmem((8, rows), F32), vmem((NY, 8, rows), F32),
        vmem((2, kz, 2, half, width), BF16), vmem((2, kz, 2, half, width), BF16),
        vmem((2, ky, 2, half, width), BF16), vmem((2, ky, 2, half, width), BF16),
        vmem((nl, per, width), BF16), vmem((nl, per, width), BF16),
        dma((nl,)), dma((nl,)), dma((2, kz, 2)), dma((nz, 2)), dma((2, ky, 2)), dma((NY, 2)),
        dma((nz,)), dma((nz,)), dma((NY,)), dma((NY,)), dma((nz,)), dma((nz,)), dma((NY,)), dma((NY,)),
        dma((2, kz, 2)), dma((2, kz, 2)), dma((2, ky, 2)), dma((2, ky, 2)), dma((nl,)), dma((nl,)),
    ]
    return tuple(
        pl.pallas_call(
            kernel,
            out_shape=(
                jax.ShapeDtypeStruct((rows, width), BF16),
                jax.ShapeDtypeStruct((nl, per, width), BF16),
                jax.ShapeDtypeStruct((1,), F32),
            ),
            in_specs=[in_smem, in_smem, in_smem, in_vmem, in_vmem, in_vmem],
            out_specs=(in_vmem, in_vmem, in_smem),
            scratch_shapes=scratch,
            compiler_params=pltpu.CompilerParams(
                collective_id=0, has_side_effects=True, vmem_limit_bytes=48 << 20
            ),
        )(slot_group, counts, pair_weight, align, src_emb, tgt_emb)
    )


def solution(mesh):
    in_specs = (
        P(("lang", "dp"), None),
        P(None, ("lang", "dp"), None),
        P(),
        P(),
        P("lang", None),
        P(),
    )
    out_specs = (P(("lang", "dp"), None), P(None, ("lang", "dp"), None), P("lang"))
    return jax.shard_map(
        per_device, mesh=mesh, in_specs=in_specs, out_specs=out_specs, check_vma=False
    )
```

time: 612 us -> 66.7 us (0.11)
  the two profiles are of different devices: /device:TPU:2 before, /device:TPU:1 now
where the time goes in v1:
time: 66.7 us; the launch traced here: 66.5 us
  Pallas kernels  58.2 us (87%)
  local copies, waits for them, and re-layouts  5.88 us (9%)
  between operations  2.47 us (4%)
    pallas_call x1, Pallas kernels, per_device(): pl.pallas_call(kernel, out_shape=(jax.ShapeDtypeStruct((rows, width), BF1...  58.2 us
    unnamed x14, local copies, waits for them, and re-layouts  5.88 us

profile of v1, /device:TPU:1, one launch (start us, length us, event | category | flops | bytes accessed | tf_op | source)
XLA Modules:
  0.0 66.5 jit_solution(10298812891554295526)
XLA Ops:
  0.6 0.0 copy-start
  0.6 0.9 %copy-done = bf16[128,768]{1,0:T(8,128)(2,1)S(1)} copy-done((bf16[128,768]{1,0:T(8,128)(2,1)S(1)}, bf16[128,768]{1,0:T(8,128)(2,1)}, u32[]{:S(2)}) %copy-start) | copy-done | bytes 196632
  1.6 0.0 copy-start.1
  1.6 0.9 %copy-done.1 = bf16[8,16,768]{2,1,0:T(8,128)(2,1)S(1)} copy-done((bf16[8,16,768]{2,1,0:T(8,128)(2,1)S(1)}, bf16[8,16,768]{2,1,0:T(8,128)(2,1)}, u32[]{:S(2)}) %copy-start.1) | copy-done | bytes 196632
  2.5 0.0 copy-start.2
  2.5 0.7 %copy-done.2 = s32[1,4096]{1,0:T(1,128)S(1)} copy-done((s32[1,4096]{1,0:T(1,128)S(1)}, s32[1,4096]{1,0:T(1,128)}, u32[]{:S(2)}) %copy-start.2) | copy-done | bytes 16408
  3.2 0.0 copy-start.3
  3.2 0.7 copy-done.3
  3.9 0.0 copy-start.4
  3.9 0.7 copy-done.4
  4.5 0.0 copy-start.5
  4.5 0.7 copy-done.5
  5.2 58.2 %shard_map.85 = (bf16[128,768]{1,0:T(8,128)(2,1)S(1)}, bf16[8,16,768]{2,1,0:T(8,128)(2,1)S(1)}, f32[1]{0:T(128)}) custom-call(s32[8]{0:T(128)S(1)} %copy-done.3, s32[8]{0:T(128)S(1)} %copy-done.4, f32[8]{0:T(128)S(1)} %copy-done.5, s32[1,4096]{1,0:T(1,128)S(1)} %copy-done.2, bf16[128,768]{1,0:T(8,128)(2,1)S(1)} %copy-done, bf16[8,16,768]{2,1,0:T(8,128)(2,1)S(1)} %copy-done.1), custom_call_target="tpu_custom_call" | custom-call | tf_op jit(solution)/shard_map/pallas_call | solution.py:376
  63.3 0.7 %copy.12 = bf16[128,768]{1,0:T(8,128)(2,1)} copy(bf16[128,768]{1,0:T(8,128)(2,1)S(1)} %get-tuple-element.6) | data formatting | bytes 393216
  64.0 0.7 %copy.13 = bf16[8,16,768]{2,1,0:T(8,128)(2,1)} copy(bf16[8,16,768]{2,1,0:T(8,128)(2,1)S(1)} %get-tuple-element.7) | data formatting | bytes 393216
Async XLA Ops:
  0.6 0.9 %copy-start = (bf16[128,768]{1,0:T(8,128)(2,1)S(1)}, bf16[128,768]{1,0:T(8,128)(2,1)}, u32[]{:S(2)}) copy-start(bf16[128,768]{1,0:T(8,128)(2,1)} %x.1) | copy-start | bytes 589828
  1.6 0.9 %copy-start.1 = (bf16[8,16,768]{2,1,0:T(8,128)(2,1)S(1)}, bf16[8,16,768]{2,1,0:T(8,128)(2,1)}, u32[]{:S(2)}) copy-start(bf16[8,16,768]{2,1,0:T(8,128)(2,1)} %t.1) | copy-start | bytes 589828
  2.5 0.7 %copy-start.2 = (s32[1,4096]{1,0:T(1,128)S(1)}, s32[1,4096]{1,0:T(1,128)}, u32[]{:S(2)}) copy-start(s32[1,4096]{1,0:T(1,128)} %align.1) | copy-start | bytes 49156
  3.2 0.7 copy-start.3
  3.9 0.7 copy-start.4
  4.5 0.7 copy-start.5

commit v2 on v1

--- a/solution.py
+++ b/solution.py
@@ -16,12 +16,12 @@
 
 
 def kernel(
-    slots, counts, weights, align, x, t, gsrc, gtgt, loss,
-    xs, ys, staged, acol, colok, er, ec, rmax, cmax, gm, psrc, ptgt,
+    slots_hbm, counts_hbm, weights_hbm, align_hbm, x, t_hbm, gsrc, gtgt, loss,
+    slots, counts, weights, align, t, xs, ys, staged, acol, colok, er, ec, rmax, cmax, gm, psrc, ptgt,
     rst_out, rst_in, cst_out, cst_in, lz_out, lz_in, ly_out, ly_in,
     fz_out, fz_in, fy_out, fy_in, back, ret,
     sa, ra, sgz, rgz, sgy, rgy, srs, rrs, scs, rcs, slz, rlz, sly, rly,
-    sfz, rfz, sfy, rfy, sb, rb,
+    sfz, rfz, sfy, rfy, sb, rb, fetched,
 ):
     nl, per = t.shape[0], t.shape[1]
     nz = xs.shape[0]
@@ -30,8 +30,6 @@
     inv_root = 1.0 / math.sqrt(width)
     lang, dp = lax.axis_index("lang"), lax.axis_index("dp")
     z, y = dp // NY, dp % NY
-    live = counts[lang]
-    weight = weights[lang]
 
     def z_at(k):
         return {"dp": lax.rem(z + k + nz, nz) * NY + y}
@@ -55,12 +53,24 @@
         started.append(copy)
         return copy
 
+    fetches = [
+        pltpu.make_async_copy(src, dst, fetched.at[i])
+        for i, (src, dst) in enumerate(
+            [(x, xs.at[0]), (slots_hbm, slots), (t_hbm, t), (align_hbm, align), (counts_hbm, counts), (weights_hbm, weights)]
+        )
+    ]
+
     barrier = pltpu.get_barrier_semaphore()
     peers = [z_at(k) for k in range(1, nz)] + [y_at(k) for k in range(1, NY)]
     peers += [lang_at(k) for k in range(1, nl)]
     for to in peers:
         pl.semaphore_signal(barrier, inc=1, device_id=to, device_id_type=pl.DeviceIdType.MESH)
-    xs[0] = x[...]
+    for copy in fetches:
+        copy.start()
+    for copy in fetches:
+        copy.wait()
+    live = counts[lang]
+    weight = weights[lang]
     for o in range(nl):
         group = lax.rem(lang + o, nl)
         slot = jnp.int32(0)
@@ -139,7 +149,7 @@
 
     total_pos = [jnp.zeros((1, NY * rows), F32)]
 
-    def scores(r):
+    def scores(r, group):
         raw = lax.dot_general(
             xs[r], all_targets(), (((1,), (1,)), ((), ())), preferred_element_type=F32
         )
@@ -153,7 +163,7 @@
         er[r] = e
         row_lse = top + jnp.log(jnp.sum(e, axis=1, keepdims=True))
         rmax[r] = jnp.broadcast_to(top, (rows, rows))
-        rst_out[r : r + 1] = jnp.broadcast_to(row_lse, (rows, rows)).T[0:1]
+        rst_out[group, r : r + 1] = jnp.broadcast_to(row_lse, (rows, rows)).T[0:1]
         top = jnp.max(s, axis=0, keepdims=True)
         e = jnp.exp(s - top)
         ec[r] = e
@@ -168,35 +178,48 @@
                 if (d, k + 1, part) in gz:
                     start(gz[d, k + 1, part])
 
+    row_copies = {}
+
+    def send_rows(group):
+        for k in range(1, nz):
+            row_copies[group, k] = start(
+                remote(rst_out.at[group], rst_in.at[group, k], srs.at[group, k], rrs.at[group, k], z_at(k))
+            )
+
     z_step(0, 0)
     for o in range(1, nl):
         spread[o - 1].wait_recv()
         if o == nl // 2 - 1:
             start(gy[0, 0, 0])
-            start(gy[1, 0, 0])
         if o == nl - 1:
-            start(gy[0, 0, 1])
             start(gy[1, 0, 1])
+    start(gy[0, 0, 1])
+    start(gy[1, 0, 0])
     z_step(0, 1)
     gy[0, 0, 0].wait_recv()
-    gy[1, 0, 0].wait_recv()
     start(gy[0, 1, 0])
+    gy[1, 0, 1].wait_recv()
+    start(gy[1, 1, 1])
     z_step(1, 0)
     gy[0, 0, 1].wait_recv()
-    gy[1, 0, 1].wait_recv()
-    start(gy[1, 1, 1])
+    gy[1, 0, 0].wait_recv()
     z_step(1, 1)
     gy[0, 1, 0].wait_recv()
     gy[1, 1, 1].wait_recv()
-    scores(0)
-    for k in range(2, nz // 2):
-        for r in (k - 1, nz - k + 1):
-            scores(r)
-        z_step(k, 0)
-        z_step(k, 1)
-    for r in (nz // 2 - 1, nz // 2 + 1):
-        scores(r)
-    scores(nz // 2)
+    mid = nz // 2
+    scores(0, 0)
+    z_step(2, 0)
+    for r in (1, nz - 1):
+        scores(r, 0)
+    for r in (2, nz - 2):
+        scores(r, 0)
+    send_rows(0)
+    z_step(2, 1)
+    for r in (mid - 1, mid + 1):
+        scores(r, 1)
+    send_rows(1)
+    z_step(3, 0)
+    scores(mid, 2)
 
     parts = cmax[:, 1, :]
     top = jnp.max(parts, axis=0, keepdims=True)
@@ -204,8 +227,8 @@
     for q in range(NY):
         cst_out[q : q + 1] = col_part[:, q * rows : (q + 1) * rows]
         cst_out[q + NY : q + NY + 1] = col_part[:, q * rows : (q + 1) * rows]
-    rst = [start(remote(rst_out, rst_in.at[k], srs.at[k], rrs.at[k], z_at(k))) for k in range(1, nz)]
     cst = [start(remote(cst_out, cst_in.at[k], scs.at[k], rcs.at[k], y_at(k))) for k in range(1, NY)]
+    send_rows(2)
 
     def combine(pieces):
         top = functools.reduce(jnp.maximum, pieces)
@@ -217,13 +240,31 @@
     for copy in cst:
         copy.wait_recv()
     col_lse = combine([cst_out[0:NY]] + [turn(cst_in[k, 0:NY], k) for k in range(1, NY)])
-    for copy in rst:
-        copy.wait_recv()
-    row_lse = combine([rst_out[...]] + [turn(rst_in[k], k) for k in range(1, nz)])
+
+    def group_of(r):
+        return {mid: 2, mid - 1: 1, mid + 1: 1}.get(r, 0)
+
+    arrived = set()
+    row_lses = {}
+
+    def row_lse(r):
+        if r in row_lses:
+            return row_lses[r]
+        pieces = [rst_out[group_of(r), r : r + 1]]
+        for k in range(1, nz):
+            there = (r - k) % nz
+            group = group_of(there)
+            if (group, k) not in arrived:
+                row_copies[group, k].wait_recv()
+                arrived.add((group, k))
+            pieces.append(rst_in[group, k, there : there + 1])
+        row_lses[r] = combine(pieces)
+        return row_lses[r]
+
 
     def gradient(r):
         pos, row_ok = masks(r)
-        own = jnp.broadcast_to(row_lse[r : r + 1], (rows, rows)).T
+        own = jnp.broadcast_to(row_lse(r), (rows, rows)).T
         by_row = jnp.where(row_ok, weight * jnp.exp(rmax[r] - own), 0.0)
         for q in range(NY):
             at = slice(q * rows, (q + 1) * rows)
@@ -274,7 +315,6 @@
 
     z_send, z_owned = ring(psrc, nz, fz_out, fz_in, sfz, rfz, z_at)
     y_send, y_owned = ring(ptgt, NY, fy_out, fy_in, sfy, rfy, y_at)
-    mid = nz // 2
     gradient(mid)
     source_part(mid)
     z_send(0, 1, 0)
@@ -284,42 +324,44 @@
         source_part(r)
     z_send(0, 2, 1)
     z_send(1, 2, 0)
-    for r in range(nz):
-        if abs(r - mid) > 1:
-            gradient(r)
+    for r in (mid + 2, mid - 2):
+        gradient(r)
+        source_part(r)
+    z_send(0, 2, 0)
+    z_send(1, 2, 1)
+    for r in (mid + 3, mid - 3, 0):
+        gradient(r)
     target_part(NY // 2)
     y_send(0, 1, 0)
     y_send(1, 1, 1)
-    z_send(0, 2, 0)
-    z_send(1, 2, 1)
+    z_send(0, 3, 1)
+    z_send(1, 3, 0)
     for q in (1, 3):
         target_part(q)
     y_send(0, 2, 1)
     y_send(1, 2, 0)
-    for r in (mid + 2, mid - 2):
+    for r in (mid + 3, mid - 3):
         source_part(r)
-    z_send(0, 3, 1)
-    z_send(1, 3, 0)
+    z_send(0, 3, 0)
+    z_send(1, 3, 1)
     y_send(0, 2, 0)
     y_send(1, 2, 1)
     target_part(0)
-
-    own_rows = jnp.where(lane + first_row(0) < live, row_lse[0:1], 0.0)
+    source_part(0)
+
+    own_rows = jnp.where(lane + first_row(0) < live, row_lse(0), 0.0)
     own_cols = jnp.where(colok[0:1] > 0.5, col_lse[0:1], 0.0)
     pos_sum = functools.reduce(jnp.add, [total_pos[0][:, q * rows : (q + 1) * rows] for q in range(NY)])
     lz_out[...] = jnp.broadcast_to(own_rows + own_cols - 2.0 * pos_sum, lz_out.shape)
     lz = [start(remote(lz_out, lz_in.at[k], slz.at[k], rlz.at[k], z_at(k))) for k in range(1, nz)]
-    for r in (mid + 3, mid - 3):
-        source_part(r % nz)
-    source_part(0)
-    z_send(0, 3, 0)
-    z_send(1, 3, 1)
+    z_send(0, 4, 1)
+    z_send(1, 4, 0)
     for copy in lz:
         copy.wait_recv()
     ly_out[...] = functools.reduce(jnp.add, [lz_out[...]] + [lz_in[k] for k in range(1, nz)])
     ly = [start(remote(ly_out, ly_in.at[k], sly.at[k], rly.at[k], y_at(k))) for k in range(1, NY)]
-    z_send(0, 4, 1)
-    z_send(1, 4, 0)
+    z_send(0, 4, 0)
+    z_send(1, 4, 1)
 
     backs = []
     for h in (0, 1):
@@ -331,8 +373,6 @@
             else:
                 back[o] = value[i * per : (i + 1) * per]
                 backs.append(start(remote(back.at[o], ret.at[o], sb.at[o], rb.at[o], lang_at(-o))))
-    z_send(0, 4, 0)
-    z_send(1, 4, 1)
     for copy in ly:
         copy.wait_recv()
     everything = functools.reduce(jnp.add, [ly_out[...]] + [ly_in[k] for k in range(1, NY)])
@@ -358,19 +398,21 @@
     vmem, smem, dma = pltpu.VMEM, pltpu.SMEM, pltpu.SemaphoreType.DMA
     in_vmem, in_smem = pl.BlockSpec(memory_space=vmem), pl.BlockSpec(memory_space=smem)
     scratch = [
+        smem((nl,), jnp.int32), smem((nl,), jnp.int32), smem((nl,), F32),
+        vmem((1, nd * rows), jnp.int32), vmem((nl, per, width), BF16),
         vmem((nz, rows, width), BF16), vmem((NY, rows, width), BF16), vmem((nl, per, width), BF16),
         vmem((nz, rows, rows), F32), vmem((8, rows), F32),
         vmem((nz, rows, cols), F32), vmem((nz, rows, cols), F32),
         vmem((nz, rows, rows), F32), vmem((nz, 8, cols), F32),
         vmem((nz, rows, cols), BF16), vmem((nz, rows, width), F32), vmem((NY, rows, width), F32),
-        vmem((nz, rows), F32), vmem((nz, nz, rows), F32), vmem((8, rows), F32), vmem((NY, 8, rows), F32),
+        vmem((3, nz, rows), F32), vmem((3, nz, nz, rows), F32), vmem((8, rows), F32), vmem((NY, 8, rows), F32),
         vmem((8, rows), F32), vmem((nz, 8, rows), F32), vmem((8, rows), F32), vmem((NY, 8, rows), F32),
         vmem((2, kz, 2, half, width), BF16), vmem((2, kz, 2, half, width), BF16),
         vmem((2, ky, 2, half, width), BF16), vmem((2, ky, 2, half, width), BF16),
         vmem((nl, per, width), BF16), vmem((nl, per, width), BF16),
         dma((nl,)), dma((nl,)), dma((2, kz, 2)), dma((nz, 2)), dma((2, ky, 2)), dma((NY, 2)),
-        dma((nz,)), dma((nz,)), dma((NY,)), dma((NY,)), dma((nz,)), dma((nz,)), dma((NY,)), dma((NY,)),
-        dma((2, kz, 2)), dma((2, kz, 2)), dma((2, ky, 2)), dma((2, ky, 2)), dma((nl,)), dma((nl,)),
+        dma((3, nz)), dma((3, nz)), dma((NY,)), dma((NY,)), dma((nz,)), dma((nz,)), dma((NY,)), dma((NY,)),
+        dma((2, kz, 2)), dma((2, kz, 2)), dma((2, ky, 2)), dma((2, ky, 2)), dma((nl,)), dma((nl,)), dma((6,)),
     ]
     return tuple(
         pl.pallas_call(
@@ -380,7 +422,7 @@
                 jax.ShapeDtypeStruct((nl, per, width), BF16),
                 jax.ShapeDtypeStruct((1,), F32),
             ),
-            in_specs=[in_smem, in_smem, in_smem, in_vmem, in_vmem, in_vmem],
+            in_specs=[pl.BlockSpec(memory_space=pltpu.HBM)] * 6,
             out_specs=(in_vmem, in_vmem, in_smem),
             scratch_shapes=scratch,
             compiler_params=pltpu.CompilerParams(

time: 66.7 us -> 66.4 us (level)
  no operation moved by 1% of the time
where the time goes in v2:
time: 66.4 us; the launch traced here: 66.2 us
  Pallas kernels  57.8 us (87%)
  local copies, waits for them, and re-layouts  5.88 us (9%)
  between operations  2.47 us (4%)
    pallas_call x1, Pallas kernels, per_device(): pl.pallas_call(kernel, out_shape=(jax.ShapeDtypeStruct((rows, width), BF1...  57.8 us
    unnamed x14, local copies, waits for them, and re-layouts  5.88 us

profile of v2, /device:TPU:1, one launch (start us, length us, event | category | flops | bytes accessed | tf_op | source)
XLA Modules:
  0.0 66.2 jit_solution(990876618440917162)
XLA Ops:
  0.6 0.0 copy-start
  0.6 0.9 %copy-done = bf16[128,768]{1,0:T(8,128)(2,1)S(1)} copy-done((bf16[128,768]{1,0:T(8,128)(2,1)S(1)}, bf16[128,768]{1,0:T(8,128)(2,1)}, u32[]{:S(2)}) %copy-start) | copy-done | bytes 196632
  1.6 0.0 copy-start.1
  1.6 0.9 %copy-done.1 = bf16[8,16,768]{2,1,0:T(8,128)(2,1)S(1)} copy-done((bf16[8,16,768]{2,1,0:T(8,128)(2,1)S(1)}, bf16[8,16,768]{2,1,0:T(8,128)(2,1)}, u32[]{:S(2)}) %copy-start.1) | copy-done | bytes 196632
  2.5 0.0 copy-start.2
  2.5 0.7 %copy-done.2 = s32[1,4096]{1,0:T(1,128)S(1)} copy-done((s32[1,4096]{1,0:T(1,128)S(1)}, s32[1,4096]{1,0:T(1,128)}, u32[]{:S(2)}) %copy-start.2) | copy-done | bytes 16408
  3.2 0.0 copy-start.3
  3.2 0.7 copy-done.3
  3.9 0.0 copy-start.4
  3.9 0.7 copy-done.4
  4.5 0.0 copy-start.5
  4.5 0.7 copy-done.5
  5.2 57.8 %shard_map.85 = (bf16[128,768]{1,0:T(8,128)(2,1)S(1)}, bf16[8,16,768]{2,1,0:T(8,128)(2,1)S(1)}, f32[1]{0:T(128)}) custom-call(s32[8]{0:T(128)S(1)} %copy-done.3, s32[8]{0:T(128)S(1)} %copy-done.4, f32[8]{0:T(128)S(1)} %copy-done.5, s32[1,4096]{1,0:T(1,128)S(1)} %copy-done.2, bf16[128,768]{1,0:T(8,128)(2,1)S(1)} %copy-done, bf16[8,16,768]{2,1,0:T(8,128)(2,1)S(1)} %copy-done.1), custom_call_target="tpu_custom_call" | custom-call | tf_op jit(solution)/shard_map/pallas_call | solution.py:418
  63.0 0.7 %copy.12 = bf16[128,768]{1,0:T(8,128)(2,1)} copy(bf16[128,768]{1,0:T(8,128)(2,1)S(1)} %get-tuple-element.6) | data formatting | bytes 393216
  63.7 0.7 %copy.13 = bf16[8,16,768]{2,1,0:T(8,128)(2,1)} copy(bf16[8,16,768]{2,1,0:T(8,128)(2,1)S(1)} %get-tuple-element.7) | data formatting | bytes 393216
Async XLA Ops:
  0.6 0.9 %copy-start = (bf16[128,768]{1,0:T(8,128)(2,1)S(1)}, bf16[128,768]{1,0:T(8,128)(2,1)}, u32[]{:S(2)}) copy-start(bf16[128,768]{1,0:T(8,128)(2,1)} %x.1) | copy-start | bytes 589828
  1.6 0.9 %copy-start.1 = (bf16[8,16,768]{2,1,0:T(8,128)(2,1)S(1)}, bf16[8,16,768]{2,1,0:T(8,128)(2,1)}, u32[]{:S(2)}) copy-start(bf16[8,16,768]{2,1,0:T(8,128)(2,1)} %t_hbm.1) | copy-start | bytes 589828
  2.5 0.7 %copy-start.2 = (s32[1,4096]{1,0:T(1,128)S(1)}, s32[1,4096]{1,0:T(1,128)}, u32[]{:S(2)}) copy-start(s32[1,4096]{1,0:T(1,128)} %align_hbm.1) | copy-start | bytes 49156
  3.2 0.7 copy-start.3
  3.9 0.7 copy-start.4
  4.5 0.7 copy-start.5

commit v3 on v2

--- a/solution.py
+++ b/solution.py
@@ -37,8 +37,8 @@
     def y_at(k):
         return {"dp": z * NY + lax.rem(y + k + NY, NY)}
 
-    def lang_at(k):
-        return {"lang": lax.rem(lang + k + nl, nl)}
+    def lang_at(p):
+        return {"lang": lang ^ p}
 
     def remote(src, dst, send, recv, to):
         return pltpu.make_async_remote_copy(
@@ -67,50 +67,57 @@
         pl.semaphore_signal(barrier, inc=1, device_id=to, device_id_type=pl.DeviceIdType.MESH)
     for copy in fetches:
         copy.start()
-    for copy in fetches:
+    pl.semaphore_wait(barrier, len(peers))
+
+    def gather_copies(first, buf, n, onward, send, recv, at):
+        copies = {}
+        chunks = len(onward[0]) + len(onward[1])
+        size = rows // chunks
+        for d in (0, 1):
+            for k in range(n // 2):
+                for c in range(chunks) if k < n // 2 - 1 else onward[d]:
+                    part = pl.ds(c * size, size)
+                    src, dst = (k, k + 1) if d == 0 else ((n - k) % n, n - 1 - k)
+                    copies[d, k, c] = remote(
+                        (buf.at[src] if k else first).at[part], buf.at[dst, part],
+                        send.at[d, k, c], recv.at[dst, c], at(1 - 2 * d),
+                    )
+        return copies
+
+    gz = gather_copies(x, xs, nz, ((0,), (1,)), sgz, rgz, z_at)
+    for h in (0, 1):
+        start(gz[0, 0, h])
+        start(gz[1, 0, 1 - h])
+
+    for copy in fetches[1:3]:
+        copy.wait()
+    for p in range(nl):
+        group = lang ^ p
+        slot = jnp.int32(0)
+        for s in range(nl):
+            slot = jnp.where(slots[s] == group, s, slot)
+        if p == 0:
+            ys[0, 0:per] = t[slot]
+        else:
+            staged[p] = t[slot]
+    spread = {
+        p: start(remote(staged.at[p], ys.at[0, pl.ds(p * per, per)], sa.at[p], ra.at[p], lang_at(p)))
+        for p in (1, 4, 5, 2, 6, 3, 7)
+    }
+    gy = gather_copies(ys.at[0], ys, NY, ((0, 2), (1, 3)), sgy, rgy, y_at)
+    spread[1].wait_recv()
+    for d in (0, 1):
+        start(gy[d, 0, 0])
+    for copy in fetches[0:1] + fetches[3:]:
         copy.wait()
     live = counts[lang]
     weight = weights[lang]
-    for o in range(nl):
-        group = lax.rem(lang + o, nl)
-        slot = jnp.int32(0)
-        for s in range(nl):
-            slot = jnp.where(slots[s] == group, s, slot)
-        staged[o] = t[slot]
-    ys[0, 0:per] = staged[0]
-    pl.semaphore_wait(barrier, len(peers))
-
-    def gather_copies(buf, n, send, recv, at):
-        copies = {}
-        for k in range(n // 2):
-            for h in (0, 1):
-                part = pl.ds(h * half, half)
-                if k < n // 2 - 1 or h == 0:
-                    copies[0, k, h] = remote(
-                        buf.at[k, part], buf.at[k + 1, part], send.at[0, k, h], recv.at[k + 1, h], at(1)
-                    )
-                if k < n // 2 - 1 or h == 1:
-                    copies[1, k, h] = remote(
-                        buf.at[(n - k) % n, part], buf.at[n - 1 - k, part],
-                        send.at[1, k, h], recv.at[n - 1 - k, h], at(-1),
-                    )
-        return copies
-
-    gz = gather_copies(xs, nz, sgz, rgz, z_at)
-    gy = gather_copies(ys, NY, sgy, rgy, y_at)
-    for h in (0, 1):
-        start(gz[0, 0, h])
-        start(gz[1, 0, 1 - h])
-    spread = [
-        start(remote(staged.at[o], ys.at[0, pl.ds(o * per, per)], sa.at[o], ra.at[o], lang_at(o)))
-        for o in range(1, nl)
-    ]
 
     lane = lax.broadcasted_iota(jnp.int32, (1, rows), 1)
     sub = lax.broadcasted_iota(jnp.int32, (rows, rows), 0)
 
     def target_of(q, position):
-        source = lax.rem(lang - position // per + nl, nl)
+        source = lang ^ (position // per)
         return (source * (nz * NY) + z * NY + lax.rem(y - q + NY, NY)) * per + position % per
 
     def first_row(r):
@@ -186,26 +193,33 @@
                 remote(rst_out.at[group], rst_in.at[group, k], srs.at[group, k], rrs.at[group, k], z_at(k))
             )
 
+    def y_begin(c):
+        for p in (2 * c, 2 * c + 1):
+            spread[p].wait_recv()
+        for d in (0, 1):
+            start(gy[d, 0, c])
+
+    def y_on(d, c):
+        gy[d, 0, c].wait_recv()
+        start(gy[d, 1, c])
+
+    y_begin(1)
+    y_begin(3)
     z_step(0, 0)
-    for o in range(1, nl):
-        spread[o - 1].wait_recv()
-        if o == nl // 2 - 1:
-            start(gy[0, 0, 0])
-        if o == nl - 1:
-            start(gy[1, 0, 1])
-    start(gy[0, 0, 1])
-    start(gy[1, 0, 0])
+    y_begin(2)
+    y_on(0, 0)
+    y_on(1, 1)
     z_step(0, 1)
-    gy[0, 0, 0].wait_recv()
-    start(gy[0, 1, 0])
-    gy[1, 0, 1].wait_recv()
-    start(gy[1, 1, 1])
+    y_on(1, 3)
+    y_on(0, 2)
     z_step(1, 0)
-    gy[0, 0, 1].wait_recv()
-    gy[1, 0, 0].wait_recv()
+    for d in (0, 1):
+        for c in (1 - d, 3 - d):
+            gy[d, 0, c].wait_recv()
     z_step(1, 1)
-    gy[0, 1, 0].wait_recv()
-    gy[1, 1, 1].wait_recv()
+    for d in (0, 1):
+        for c in (d, d + 2):
+            gy[d, 1, c].wait_recv()
     mid = nz // 2
     scores(0, 0)
     z_step(2, 0)
@@ -367,12 +381,12 @@
     for h in (0, 1):
         value = y_owned(h)
         for i in range(nl // 2):
-            o = h * (nl // 2) + i
-            if o == 0:
+            p = h * (nl // 2) + i
+            if p == 0:
                 ret[0] = value[0:per]
             else:
-                back[o] = value[i * per : (i + 1) * per]
-                backs.append(start(remote(back.at[o], ret.at[o], sb.at[o], rb.at[o], lang_at(-o))))
+                back[p] = value[i * per : (i + 1) * per]
+                backs.append(start(remote(back.at[p], ret.at[p], sb.at[p], rb.at[p], lang_at(p))))
     for copy in ly:
         copy.wait_recv()
     everything = functools.reduce(jnp.add, [ly_out[...]] + [ly_in[k] for k in range(1, NY)])
@@ -380,7 +394,7 @@
     for copy in backs:
         copy.wait_recv()
     for s in range(nl):
-        gtgt[s] = ret[lax.rem(slots[s] - lang + nl, nl)]
+        gtgt[s] = ret[slots[s] ^ lang]
     for h in (1, 0):
         gsrc[h * half : (h + 1) * half] = z_owned(h)
     for copy in started:
@@ -410,7 +424,7 @@
         vmem((2, kz, 2, half, width), BF16), vmem((2, kz, 2, half, width), BF16),
         vmem((2, ky, 2, half, width), BF16), vmem((2, ky, 2, half, width), BF16),
         vmem((nl, per, width), BF16), vmem((nl, per, width), BF16),
-        dma((nl,)), dma((nl,)), dma((2, kz, 2)), dma((nz, 2)), dma((2, ky, 2)), dma((NY, 2)),
+        dma((nl,)), dma((nl,)), dma((2, kz, 2)), dma((nz, 2)), dma((2, ky, 4)), dma((NY, 4)),
         dma((3, nz)), dma((3, nz)), dma((NY,)), dma((NY,)), dma((nz,)), dma((nz,)), dma((NY,)), dma((NY,)),
         dma((2, kz, 2)), dma((2, kz, 2)), dma((2, ky, 2)), dma((2, ky, 2)), dma((nl,)), dma((nl,)), dma((6,)),
     ]
@@ -422,11 +436,11 @@
                 jax.ShapeDtypeStruct((nl, per, width), BF16),
                 jax.ShapeDtypeStruct((1,), F32),
             ),
-            in_specs=[pl.BlockSpec(memory_space=pltpu.HBM)] * 6,
+            in_specs=[pl.BlockSpec(memory_space=pl.ANY)] * 6,
             out_specs=(in_vmem, in_vmem, in_smem),
             scratch_shapes=scratch,
             compiler_params=pltpu.CompilerParams(
-                collective_id=0, has_side_effects=True, vmem_limit_bytes=48 << 20
+                collective_id=0, has_side_effects=True, vmem_limit_bytes=58 << 20
             ),
         )(slot_group, counts, pair_weight, align, src_emb, tgt_emb)
     )

time: 66.4 us -> 63.2 us (0.952)
  local copies, waits for them, and re-layouts: 5.88 us -> 2.34 us
    unnamed x14 -> x4, local copies, waits for them, and re-layouts: 5.88 us -> 2.34 us
where the time goes in v3:
time: 63.2 us; the launch traced here: 63.1 us
  Pallas kernels  58.3 us (92%)
  between operations  2.47 us (4%)
  local copies, waits for them, and re-layouts  2.34 us (4%)
    pallas_call x1, Pallas kernels, per_device(): pl.pallas_call(kernel, out_shape=(jax.ShapeDtypeStruct((rows, width), BF1...  58.3 us
    unnamed x4, local copies, waits for them, and re-layouts  2.34 us

profile of v3, /device:TPU:1, one launch (start us, length us, event | category | flops | bytes accessed | tf_op | source)
XLA Modules:
  0.0 63.1 jit_solution(16475966154840674062)
XLA Ops:
  0.6 58.3 %shard_map.85 = (bf16[128,768]{1,0:T(8,128)(2,1)}, bf16[8,16,768]{2,1,0:T(8,128)(2,1)}, f32[1]{0:T(128)}) custom-call(s32[8]{0:T(128)} %slots_hbm.1, s32[8]{0:T(128)} %counts_hbm.1, f32[8]{0:T(128)} %weights_hbm.1, s32[1,4096]{1,0:T(1,128)} %align_hbm.1, bf16[128,768]{1,0:T(8,128)(2,1)} %x.1, bf16[8,16,768]{2,1,0:T(8,128)(2,1)} %t_hbm.1), custom_call_target="tpu_custom_call" | custom-call | tf_op jit(solution)/shard_map/pallas_call | solution.py:432
  58.9 0.0 copy-start
  59.0 1.7 %copy.12 = bf16[128,768]{1,0:T(8,128)(2,1)} copy(bf16[128,768]{1,0:T(8,128)(2,1)} %get-tuple-element.6) | data formatting | bytes 393216
  60.6 0.0 copy-done
  60.6 0.7 %copy.13 = bf16[8,16,768]{2,1,0:T(8,128)(2,1)} copy(bf16[8,16,768]{2,1,0:T(8,128)(2,1)S(1)} %copy-done) | data formatting | bytes 393216
Async XLA Ops:
  58.9 1.7 %copy-start = (bf16[8,16,768]{2,1,0:T(8,128)(2,1)S(1)}, bf16[8,16,768]{2,1,0:T(8,128)(2,1)}, u32[]{:S(2)}) copy-start(bf16[8,16,768]{2,1,0:T(8,128)(2,1)} %get-tuple-element.7) | copy-start | bytes 589828

commit v4 on v3

--- a/solution.py
+++ b/solution.py
@@ -20,8 +20,7 @@
     slots, counts, weights, align, t, xs, ys, staged, acol, colok, er, ec, rmax, cmax, gm, psrc, ptgt,
     rst_out, rst_in, cst_out, cst_in, lz_out, lz_in, ly_out, ly_in,
     fz_out, fz_in, fy_out, fy_in, back, ret,
-    sa, ra, sgz, rgz, sgy, rgy, srs, rrs, scs, rcs, slz, rlz, sly, rly,
-    sfz, rfz, sfy, rfy, sb, rb, fetched,
+    sends, ra, rgz, rgy, rrs, rcs, rls, rfz, rfy, fetched,
 ):
     nl, per = t.shape[0], t.shape[1]
     nz = xs.shape[0]
@@ -46,12 +45,12 @@
             device_id=to, device_id_type=pl.DeviceIdType.MESH,
         )
 
-    started = []
-
     def start(copy):
         copy.start()
-        started.append(copy)
         return copy
+
+    def wait_for(ref, sem):
+        pltpu.make_async_copy(ref, ref, sem).wait()
 
     fetches = [
         pltpu.make_async_copy(src, dst, fetched.at[i])
@@ -80,11 +79,11 @@
                     src, dst = (k, k + 1) if d == 0 else ((n - k) % n, n - 1 - k)
                     copies[d, k, c] = remote(
                         (buf.at[src] if k else first).at[part], buf.at[dst, part],
-                        send.at[d, k, c], recv.at[dst, c], at(1 - 2 * d),
+                        send, recv.at[dst, c], at(1 - 2 * d),
                     )
         return copies
 
-    gz = gather_copies(x, xs, nz, ((0,), (1,)), sgz, rgz, z_at)
+    gz = gather_copies(x, xs, nz, ((0,), (1,)), sends.at[0], rgz, z_at)
     for h in (0, 1):
         start(gz[0, 0, h])
         start(gz[1, 0, 1 - h])
@@ -100,12 +99,10 @@
             ys[0, 0:per] = t[slot]
         else:
             staged[p] = t[slot]
-    spread = {
-        p: start(remote(staged.at[p], ys.at[0, pl.ds(p * per, per)], sa.at[p], ra.at[p], lang_at(p)))
-        for p in (1, 4, 5, 2, 6, 3, 7)
-    }
-    gy = gather_copies(ys.at[0], ys, NY, ((0, 2), (1, 3)), sgy, rgy, y_at)
-    spread[1].wait_recv()
+    for p in (1, 4, 5, 2, 6, 3, 7):
+        start(remote(staged.at[p], ys.at[0, pl.ds(p * per, per)], sends.at[2], ra.at[p // 2], lang_at(p)))
+    gy = gather_copies(ys.at[0], ys, NY, ((0, 2), (1, 3)), sends.at[1], rgy, y_at)
+    wait_for(ys.at[0, pl.ds(per, per)], ra.at[0])
     for d in (0, 1):
         start(gy[d, 0, 0])
     for copy in fetches[0:1] + fetches[3:]:
@@ -185,17 +182,16 @@
                 if (d, k + 1, part) in gz:
                     start(gz[d, k + 1, part])
 
-    row_copies = {}
+    def rows_from(group, k):
+        return 0 if group < 2 else min(k, nz - k)
 
     def send_rows(group):
         for k in range(1, nz):
-            row_copies[group, k] = start(
-                remote(rst_out.at[group], rst_in.at[group, k], srs.at[group, k], rrs.at[group, k], z_at(k))
-            )
+            recv = rrs.at[rows_from(group, k)]
+            start(remote(rst_out.at[group], rst_in.at[group, k], sends.at[3], recv, z_at(k)))
 
     def y_begin(c):
-        for p in (2 * c, 2 * c + 1):
-            spread[p].wait_recv()
+        wait_for(ys.at[0, pl.ds(2 * c * per, 2 * per)], ra.at[c])
         for d in (0, 1):
             start(gy[d, 0, c])
 
@@ -204,15 +200,15 @@
         start(gy[d, 1, c])
 
     y_begin(1)
+    z_step(0, 0)
     y_begin(3)
-    z_step(0, 0)
+    z_step(0, 1)
     y_begin(2)
     y_on(0, 0)
     y_on(1, 1)
-    z_step(0, 1)
+    z_step(1, 0)
     y_on(1, 3)
     y_on(0, 2)
-    z_step(1, 0)
     for d in (0, 1):
         for c in (1 - d, 3 - d):
             gy[d, 0, c].wait_recv()
@@ -241,7 +237,8 @@
     for q in range(NY):
         cst_out[q : q + 1] = col_part[:, q * rows : (q + 1) * rows]
         cst_out[q + NY : q + NY + 1] = col_part[:, q * rows : (q + 1) * rows]
-    cst = [start(remote(cst_out, cst_in.at[k], scs.at[k], rcs.at[k], y_at(k))) for k in range(1, NY)]
+    for k in range(1, NY):
+        start(remote(cst_out, cst_in.at[k], sends.at[4], rcs.at[0], y_at(k)))
     send_rows(2)
 
     def combine(pieces):
@@ -251,8 +248,7 @@
     def turn(piece, k):
         return jnp.concatenate([piece[piece.shape[0] - k :], piece[: piece.shape[0] - k]], axis=0)
 
-    for copy in cst:
-        copy.wait_recv()
+    wait_for(cst_in.at[1:NY], rcs.at[0])
     col_lse = combine([cst_out[0:NY]] + [turn(cst_in[k, 0:NY], k) for k in range(1, NY)])
 
     def group_of(r):
@@ -268,9 +264,11 @@
         for k in range(1, nz):
             there = (r - k) % nz
             group = group_of(there)
-            if (group, k) not in arrived:
-                row_copies[group, k].wait_recv()
-                arrived.add((group, k))
+            which = rows_from(group, k)
+            if which not in arrived:
+                arrived.add(which)
+                together = {0: rst_in.at[0:2, 1:nz], nz // 2: rst_in.at[2, 1:2]}
+                wait_for(together.get(which, rst_in.at[2, 1:3]), rrs.at[which])
             pieces.append(rst_in[group, k, there : there + 1])
         row_lses[r] = combine(pieces)
         return row_lses[r]
@@ -315,7 +313,7 @@
                 value = value + inn[d, k - 1, h].astype(F32)
             out[d, k, h] = value.astype(BF16)
             copies[d, k, h] = start(
-                remote(out.at[d, k, h], inn.at[d, k, h], send.at[d, k, h], recv.at[d, k, h], at(1 if d == 0 else -1))
+                remote(out.at[d, k, h], inn.at[d, k, h], send, recv.at[d, k - 1, h], at(1 - 2 * d))
             )
 
         def owned(h):
@@ -327,8 +325,8 @@
 
         return step, owned
 
-    z_send, z_owned = ring(psrc, nz, fz_out, fz_in, sfz, rfz, z_at)
-    y_send, y_owned = ring(ptgt, NY, fy_out, fy_in, sfy, rfy, y_at)
+    z_send, z_owned = ring(psrc, nz, fz_out, fz_in, sends.at[5], rfz, z_at)
+    y_send, y_owned = ring(ptgt, NY, fy_out, fy_in, sends.at[6], rfy, y_at)
     gradient(mid)
     source_part(mid)
     z_send(0, 1, 0)
@@ -338,47 +336,37 @@
         source_part(r)
     z_send(0, 2, 1)
     z_send(1, 2, 0)
-    for r in (mid + 2, mid - 2):
-        gradient(r)
-        source_part(r)
-    z_send(0, 2, 0)
-    z_send(1, 2, 1)
-    for r in (mid + 3, mid - 3, 0):
+    for r in (mid + 2, mid - 2, mid + 3, mid - 3, 0):
         gradient(r)
     target_part(NY // 2)
     y_send(0, 1, 0)
     y_send(1, 1, 1)
-    z_send(0, 3, 1)
-    z_send(1, 3, 0)
+    z_send(0, 2, 0)
+    z_send(1, 2, 1)
     for q in (1, 3):
         target_part(q)
     y_send(0, 2, 1)
     y_send(1, 2, 0)
-    for r in (mid + 3, mid - 3):
+    for r in (mid + 2, mid - 2):
         source_part(r)
-    z_send(0, 3, 0)
-    z_send(1, 3, 1)
+    z_send(0, 3, 1)
+    z_send(1, 3, 0)
     y_send(0, 2, 0)
     y_send(1, 2, 1)
     target_part(0)
-    source_part(0)
 
     own_rows = jnp.where(lane + first_row(0) < live, row_lse(0), 0.0)
     own_cols = jnp.where(colok[0:1] > 0.5, col_lse[0:1], 0.0)
     pos_sum = functools.reduce(jnp.add, [total_pos[0][:, q * rows : (q + 1) * rows] for q in range(NY)])
     lz_out[...] = jnp.broadcast_to(own_rows + own_cols - 2.0 * pos_sum, lz_out.shape)
-    lz = [start(remote(lz_out, lz_in.at[k], slz.at[k], rlz.at[k], z_at(k))) for k in range(1, nz)]
-    z_send(0, 4, 1)
-    z_send(1, 4, 0)
-    for copy in lz:
-        copy.wait_recv()
-    ly_out[...] = functools.reduce(jnp.add, [lz_out[...]] + [lz_in[k] for k in range(1, nz)])
-    ly = [start(remote(ly_out, ly_in.at[k], sly.at[k], rly.at[k], y_at(k))) for k in range(1, NY)]
-    z_send(0, 4, 0)
-    z_send(1, 4, 1)
-
-    backs = []
-    for h in (0, 1):
+    for k in range(1, nz):
+        start(remote(lz_out, lz_in.at[k], sends.at[7], rls.at[0], z_at(k)))
+    z_send(0, 3, 0)
+    z_send(1, 3, 1)
+    for r in (mid + 3, mid - 3):
+        source_part(r)
+
+    def send_back(h):
         value = y_owned(h)
         for i in range(nl // 2):
             p = h * (nl // 2) + i
@@ -386,19 +374,31 @@
                 ret[0] = value[0:per]
             else:
                 back[p] = value[i * per : (i + 1) * per]
-                backs.append(start(remote(back.at[p], ret.at[p], sb.at[p], rb.at[p], lang_at(p))))
-    for copy in ly:
-        copy.wait_recv()
+                start(remote(back.at[p], ret.at[p], sends.at[9], rls.at[2], lang_at(p)))
+
+    z_send(0, 4, 1)
+    z_send(1, 4, 0)
+    send_back(1)
+    send_back(0)
+    z_send(0, 4, 0)
+    z_send(1, 4, 1)
+    source_part(0)
+    wait_for(lz_in.at[1:nz], rls.at[0])
+    ly_out[...] = functools.reduce(jnp.add, [lz_out[...]] + [lz_in[k] for k in range(1, nz)])
+    for k in range(1, NY):
+        start(remote(ly_out, ly_in.at[k], sends.at[8], rls.at[1], y_at(k)))
+    wait_for(ly_in.at[1:NY], rls.at[1])
     everything = functools.reduce(jnp.add, [ly_out[...]] + [ly_in[k] for k in range(1, NY)])
     loss[0] = jnp.sum(everything[0:1]) / live.astype(F32)
-    for copy in backs:
-        copy.wait_recv()
+    wait_for(ret.at[1:nl], rls.at[2])
     for s in range(nl):
         gtgt[s] = ret[slots[s] ^ lang]
     for h in (1, 0):
         gsrc[h * half : (h + 1) * half] = z_owned(h)
-    for copy in started:
-        copy.wait_send()
+    sent = [xs.at[1:nz], ys.at[1:NY], staged.at[1:nl], rst_in.at[:, 1:nz], cst_in.at[1:NY]]
+    sent += [xs.at[1:nz], ys.at[1:NY], lz_in.at[1:nz], ly_in.at[1:NY], back.at[1:nl]]
+    for i, ref in enumerate(sent):
+        wait_for(ref, sends.at[i])
 
 
 def per_device(src_emb, tgt_emb, slot_group, counts, align, pair_weight):
@@ -424,16 +424,15 @@
         vmem((2, kz, 2, half, width), BF16), vmem((2, kz, 2, half, width), BF16),
         vmem((2, ky, 2, half, width), BF16), vmem((2, ky, 2, half, width), BF16),
         vmem((nl, per, width), BF16), vmem((nl, per, width), BF16),
-        dma((nl,)), dma((nl,)), dma((2, kz, 2)), dma((nz, 2)), dma((2, ky, 4)), dma((NY, 4)),
-        dma((3, nz)), dma((3, nz)), dma((NY,)), dma((NY,)), dma((nz,)), dma((nz,)), dma((NY,)), dma((NY,)),
-        dma((2, kz, 2)), dma((2, kz, 2)), dma((2, ky, 2)), dma((2, ky, 2)), dma((nl,)), dma((nl,)), dma((6,)),
+        dma((10,)), dma((4,)), dma((nz, 2)), dma((NY, 4)), dma((5,)), dma((1,)), dma((3,)),
+        dma((2, nz // 2, 2)), dma((2, NY // 2, 2)), dma((6,)),
     ]
     return tuple(
         pl.pallas_call(
             kernel,
             out_shape=(
-                jax.ShapeDtypeStruct((rows, width), BF16),
-                jax.ShapeDtypeStruct((nl, per, width), BF16),
+                pltpu.VMEM((rows, width), BF16),
+                pltpu.VMEM((nl, per, width), BF16),
                 jax.ShapeDtypeStruct((1,), F32),
             ),
             in_specs=[pl.BlockSpec(memory_space=pl.ANY)] * 6,

time: 63.2 us -> 55.5 us (0.88); the launches traced: 63.1 us -> 54.5 us
  Pallas kernels: 58.3 us -> 50.8 us
  local copies, waits for them, and re-layouts: 2.34 us -> 1.36 us
    pallas_call x1, Pallas kernels: 58.3 us -> 50.8 us  [per_device(): pl.pallas_call(kernel, out_shape=(pltpu.VMEM((rows, width), BF16), pltpu....]
    unnamed x4 -> x2, local copies, waits for them, and re-layouts: 2.34 us -> 1.36 us
where the time goes in v4:
time: 55.5 us; the launch traced here: 54.5 us
  Pallas kernels  50.8 us (92%)
  between operations  2.33 us (4%)
  local copies, waits for them, and re-layouts  1.36 us (2%)
    pallas_call x1, Pallas kernels, per_device(): pl.pallas_call(kernel, out_shape=(pltpu.VMEM((rows, width), BF16), pltpu....  50.8 us
    unnamed x2, local copies, waits for them, and re-layouts  1.36 us

profile of v4, /device:TPU:1, one launch (start us, length us, event | category | flops | bytes accessed | tf_op | source)
XLA Modules:
  0.0 54.5 jit_solution(5896455924328015474)
XLA Ops:
  0.6 50.8 %shard_map.85 = (bf16[128,768]{1,0:T(8,128)(2,1)S(1)}, bf16[8,16,768]{2,1,0:T(8,128)(2,1)S(1)}, f32[1]{0:T(128)}) custom-call(s32[8]{0:T(128)} %slots_hbm.1, s32[8]{0:T(128)} %counts_hbm.1, f32[8]{0:T(128)} %weights_hbm.1, s32[1,4096]{1,0:T(1,128)} %align_hbm.1, bf16[128,768]{1,0:T(8,128)(2,1)} %x.1, bf16[8,16,768]{2,1,0:T(8,128)(2,1)} %t_hbm.1), custom_call_target="tpu_custom_call" | custom-call | tf_op jit(solution)/shard_map/pallas_call | solution.py:431
  51.4 0.7 %copy.12 = bf16[128,768]{1,0:T(8,128)(2,1)} copy(bf16[128,768]{1,0:T(8,128)(2,1)S(1)} %get-tuple-element.3) | data formatting | bytes 393216
  52.1 0.7 %copy.13 = bf16[8,16,768]{2,1,0:T(8,128)(2,1)} copy(bf16[8,16,768]{2,1,0:T(8,128)(2,1)S(1)} %get-tuple-element.4) | data formatting | bytes 393216

commit v5 on v4

--- a/solution.py
+++ b/solution.py
@@ -389,7 +389,7 @@
         start(remote(ly_out, ly_in.at[k], sends.at[8], rls.at[1], y_at(k)))
     wait_for(ly_in.at[1:NY], rls.at[1])
     everything = functools.reduce(jnp.add, [ly_out[...]] + [ly_in[k] for k in range(1, NY)])
-    loss[0] = jnp.sum(everything[0:1]) / live.astype(F32)
+    loss[...] = jnp.broadcast_to(jnp.sum(everything[0:1], keepdims=True) / live.astype(F32), loss.shape)
     wait_for(ret.at[1:nl], rls.at[2])
     for s in range(nl):
         gtgt[s] = ret[slots[s] ^ lang]
@@ -399,6 +399,17 @@
     sent += [xs.at[1:nz], ys.at[1:NY], lz_in.at[1:nz], ly_in.at[1:NY], back.at[1:nl]]
     for i, ref in enumerate(sent):
         wait_for(ref, sends.at[i])
+
+
+def write_out(gsrc, gtgt, loss, gsrc_hbm, gtgt_hbm, loss_hbm, total, sem):
+    copies = [pltpu.make_async_copy(gsrc, gsrc_hbm, sem.at[0]), pltpu.make_async_copy(gtgt, gtgt_hbm, sem.at[1])]
+    for copy in copies:
+        copy.start()
+    total[0] = loss[0, 0]
+    copies.append(pltpu.make_async_copy(total, loss_hbm, sem.at[2]))
+    copies[2].start()
+    for copy in copies:
+        copy.wait()
 
 
 def per_device(src_emb, tgt_emb, slot_group, counts, align, pair_weight):
@@ -427,22 +438,30 @@
         dma((10,)), dma((4,)), dma((nz, 2)), dma((NY, 4)), dma((5,)), dma((1,)), dma((3,)),
         dma((2, nz // 2, 2)), dma((2, NY // 2, 2)), dma((6,)),
     ]
-    return tuple(
+    found = tuple(
         pl.pallas_call(
             kernel,
             out_shape=(
                 pltpu.VMEM((rows, width), BF16),
                 pltpu.VMEM((nl, per, width), BF16),
-                jax.ShapeDtypeStruct((1,), F32),
+                pltpu.VMEM((8, rows), F32),
             ),
             in_specs=[pl.BlockSpec(memory_space=pl.ANY)] * 6,
-            out_specs=(in_vmem, in_vmem, in_smem),
+            out_specs=(in_vmem, in_vmem, in_vmem),
             scratch_shapes=scratch,
             compiler_params=pltpu.CompilerParams(
                 collective_id=0, has_side_effects=True, vmem_limit_bytes=58 << 20
             ),
         )(slot_group, counts, pair_weight, align, src_emb, tgt_emb)
     )
+    shapes = [(src_emb.shape, BF16), (tgt_emb.shape, BF16), ((1,), F32)]
+    return pl.pallas_call(
+        write_out,
+        out_shape=tuple(jax.ShapeDtypeStruct(*shape) for shape in shapes),
+        in_specs=[in_vmem] * 3,
+        out_specs=(pl.BlockSpec(memory_space=pl.ANY),) * 3,
+        scratch_shapes=[smem((1,), F32), dma((3,))],
+    )(*(pltpu.with_memory_space_constraint(a, pltpu.VMEM) for a in found))
 
 
 def solution(mesh):

time: 55.5 us -> 52.7 us (0.950)
  between operations: 2.33 us -> 0.64 us
  local copies, waits for them, and re-layouts: 1.36 us -> 0 us
    unnamed x2 -> x0, local copies, waits for them, and re-layouts: 1.36 us -> none
    pallas_call x0 -> x1, Pallas kernels: none -> 0.78 us  [per_device(): pl.pallas_call(write_out, out_shape=tuple((jax.ShapeDtypeStruct(*shape) f...]
where the time goes in v5:
time: 52.7 us; the launch traced here: 51.7 us
  Pallas kernels  51.1 us (97%)
  between operations  0.64 us (1%)
    pallas_call x1, Pallas kernels, per_device(): pl.pallas_call(kernel, out_shape=(pltpu.VMEM((rows, width), BF16), pltpu....  50.3 us

profile of v5, /device:TPU:1, one launch (start us, length us, event | category | flops | bytes accessed | tf_op | source)
XLA Modules:
  0.0 51.7 jit_solution(814928089828761327)
XLA Ops:
  0.6 50.3 %shard_map.85 = (bf16[128,768]{1,0:T(8,128)(2,1)S(1)}, bf16[8,16,768]{2,1,0:T(8,128)(2,1)S(1)}, f32[8,128]{1,0:T(8,128)S(1)}) custom-call(s32[8]{0:T(128)} %slots_hbm.1, s32[8]{0:T(128)} %counts_hbm.1, f32[8]{0:T(128)} %weights_hbm.1, s32[1,4096]{1,0:T(1,128)} %align_hbm.1, bf16[128,768]{1,0:T(8,128)(2,1)} %x.1, bf16[8,16,768]{2,1,0:T(8,128)(2,1)} %t_hbm.1), custom_call_target="tpu_custom_call" | custom-call | tf_op jit(solution)/shard_map/pallas_call | solution.py:442
  50.9 0.8 %shard_map.86 = (bf16[128,768]{1,0:T(8,128)(2,1)}, bf16[8,16,768]{2,1,0:T(8,128)(2,1)}, f32[1]{0:T(128)}) custom-call(bf16[128,768]{1,0:T(8,128)(2,1)S(1)} %get-tuple-element.6.gsrc, bf16[8,16,768]{2,1,0:T(8,128)(2,1)S(1)} %get-tuple-element.7.gtgt, f32[8,128]{1,0:T(8,128)S(1)} %get-tuple-element.8.loss), custom_call_target="tpu_custom_call" | custom-call | tf_op jit(solution)/shard_map/pallas_call | solution.py:458

commit v6 on v5

--- a/solution.py
+++ b/solution.py
@@ -84,10 +84,13 @@
         return copies
 
     gz = gather_copies(x, xs, nz, ((0,), (1,)), sends.at[0], rgz, z_at)
-    for h in (0, 1):
-        start(gz[0, 0, h])
-        start(gz[1, 0, 1 - h])
-
+
+    def z_begin():
+        for h in (0, 1):
+            start(gz[0, 0, h])
+            start(gz[1, 0, 1 - h])
+
+    z_begin()
     for copy in fetches[1:3]:
         copy.wait()
     for p in range(nl):
@@ -102,9 +105,13 @@
     for p in (1, 4, 5, 2, 6, 3, 7):
         start(remote(staged.at[p], ys.at[0, pl.ds(p * per, per)], sends.at[2], ra.at[p // 2], lang_at(p)))
     gy = gather_copies(ys.at[0], ys, NY, ((0, 2), (1, 3)), sends.at[1], rgy, y_at)
-    wait_for(ys.at[0, pl.ds(per, per)], ra.at[0])
-    for d in (0, 1):
-        start(gy[d, 0, 0])
+
+    def y_first():
+        wait_for(ys.at[0, pl.ds(per, per)], ra.at[0])
+        for d in (0, 1):
+            start(gy[d, 0, 0])
+
+    y_first()
     for copy in fetches[0:1] + fetches[3:]:
         copy.wait()
     live = counts[lang]
@@ -199,6 +206,11 @@
         gy[d, 0, c].wait_recv()
         start(gy[d, 1, c])
 
+    def y_rest(k):
+        for d in (0, 1):
+            for c in (d, d + 2) if k else (1 - d, 3 - d):
+                gy[d, k, c].wait_recv()
+
     y_begin(1)
     z_step(0, 0)
     y_begin(3)
@@ -209,16 +221,13 @@
     z_step(1, 0)
     y_on(1, 3)
     y_on(0, 2)
-    for d in (0, 1):
-        for c in (1 - d, 3 - d):
-            gy[d, 0, c].wait_recv()
     z_step(1, 1)
-    for d in (0, 1):
-        for c in (d, d + 2):
-            gy[d, 1, c].wait_recv()
+    y_rest(0)
+    z_step(2, 0)
+    y_rest(1)
+
     mid = nz // 2
     scores(0, 0)
-    z_step(2, 0)
     for r in (1, nz - 1):
         scores(r, 0)
     for r in (2, nz - 2):
@@ -247,9 +256,6 @@
 
     def turn(piece, k):
         return jnp.concatenate([piece[piece.shape[0] - k :], piece[: piece.shape[0] - k]], axis=0)
-
-    wait_for(cst_in.at[1:NY], rcs.at[0])
-    col_lse = combine([cst_out[0:NY]] + [turn(cst_in[k, 0:NY], k) for k in range(1, NY)])
 
     def group_of(r):
         return {mid: 2, mid - 1: 1, mid + 1: 1}.get(r, 0)
@@ -274,18 +280,27 @@
         return row_lses[r]
 
 
-    def gradient(r):
+    def row_gradient(r):
         pos, row_ok = masks(r)
         own = jnp.broadcast_to(row_lse(r), (rows, rows)).T
         by_row = jnp.where(row_ok, weight * jnp.exp(rmax[r] - own), 0.0)
         for q in range(NY):
             at = slice(q * rows, (q + 1) * rows)
+            er[r, :, at] = er[r, :, at] * by_row - jnp.where(pos[:, at] & row_ok, 2.0 * weight, 0.0)
+
+    row_gradient(mid)
+    wait_for(cst_in.at[1:NY], rcs.at[0])
+    col_lse = combine([cst_out[0:NY]] + [turn(cst_in[k, 0:NY], k) for k in range(1, NY)])
+
+    def gradient(r):
+        if r != mid:
+            row_gradient(r)
+        for q in range(NY):
+            at = slice(q * rows, (q + 1) * rows)
             by_col = jnp.where(
                 colok[q : q + 1] > 0.5, weight * jnp.exp(cmax[r, 0:1, at] - col_lse[q : q + 1]), 0.0
             )
-            g = er[r, :, at] * by_row + ec[r, :, at] * by_col
-            g = g - jnp.where(pos[:, at] & row_ok, 2.0 * weight, 0.0)
-            gm[r, :, at] = g.astype(BF16)
+            gm[r, :, at] = (er[r, :, at] + ec[r, :, at] * by_col).astype(BF16)
 
     def source_part(r):
         psrc[r] = jnp.dot(gm[r], all_targets(), preferred_element_type=F32)

time: 52.7 us -> 52 us (0.987)
  no operation moved by 1% of the time
where the time goes in v6:
time: 52 us; the launch traced here: 51.4 us
  Pallas kernels  50.8 us (98%)
  between operations  0.64 us (1%)
    pallas_call x1, Pallas kernels, per_device(): pl.pallas_call(kernel, out_shape=(pltpu.VMEM((rows, width), BF16), pltpu....  50 us

profile of v6, /device:TPU:1, one launch (start us, length us, event | category | flops | bytes accessed | tf_op | source)
XLA Modules:
  0.0 51.4 jit_solution(4160714975913535075)
XLA Ops:
  0.6 50.0 %shard_map.85 = (bf16[128,768]{1,0:T(8,128)(2,1)S(1)}, bf16[8,16,768]{2,1,0:T(8,128)(2,1)S(1)}, f32[8,128]{1,0:T(8,128)S(1)}) custom-call(s32[8]{0:T(128)} %slots_hbm.1, s32[8]{0:T(128)} %counts_hbm.1, f32[8]{0:T(128)} %weights_hbm.1, s32[1,4096]{1,0:T(1,128)} %align_hbm.1, bf16[128,768]{1,0:T(8,128)(2,1)} %x.1, bf16[8,16,768]{2,1,0:T(8,128)(2,1)} %t_hbm.1), custom_call_target="tpu_custom_call" | custom-call | tf_op jit(solution)/shard_map/pallas_call | solution.py:457
  50.7 0.8 %shard_map.86 = (bf16[128,768]{1,0:T(8,128)(2,1)}, bf16[8,16,768]{2,1,0:T(8,128)(2,1)}, f32[1]{0:T(128)}) custom-call(bf16[128,768]{1,0:T(8,128)(2,1)S(1)} %get-tuple-element.6.gsrc, bf16[8,16,768]{2,1,0:T(8,128)(2,1)S(1)} %get-tuple-element.7.gtgt, f32[8,128]{1,0:T(8,128)S(1)} %get-tuple-element.8.loss), custom_call_target="tpu_custom_call" | custom-call | tf_op jit(solution)/shard_map/pallas_call | solution.py:473

commit v7 on v6

--- a/solution.py
+++ b/solution.py
@@ -11,6 +11,7 @@
 MARGIN = 0.3
 LOW = -1e30
 NY = 4
+CZ = 4
 F32 = jnp.float32
 BF16 = jnp.bfloat16
 
@@ -26,6 +27,7 @@
     nz = xs.shape[0]
     rows, width = x.shape
     half = rows // 2
+    cz = rgz.shape[1]
     inv_root = 1.0 / math.sqrt(width)
     lang, dp = lax.axis_index("lang"), lax.axis_index("dp")
     z, y = dp // NY, dp % NY
@@ -83,12 +85,12 @@
                     )
         return copies
 
-    gz = gather_copies(x, xs, nz, ((0,), (1,)), sends.at[0], rgz, z_at)
+    gz = gather_copies(x, xs, nz, (range(cz // 2), range(cz // 2, cz)), sends.at[0], rgz, z_at)
 
     def z_begin():
-        for h in (0, 1):
-            start(gz[0, 0, h])
-            start(gz[1, 0, 1 - h])
+        for i in range(cz):
+            start(gz[0, 0, i])
+            start(gz[1, 0, cz - 1 - i])
 
     z_begin()
     for copy in fetches[1:3]:
@@ -182,12 +184,13 @@
         cmax[r, 1:2] = top + jnp.log(jnp.sum(e, axis=0, keepdims=True))
 
     def z_step(k, h):
-        for d in (0, 1):
-            part = h if d == 0 else 1 - h
-            if (d, k, part) in gz:
-                gz[d, k, part].wait_recv()
-                if (d, k + 1, part) in gz:
-                    start(gz[d, k + 1, part])
+        for i in range(h * cz // 2, (h + 1) * cz // 2):
+            for d in (0, 1):
+                part = i if d == 0 else cz - 1 - i
+                if (d, k, part) in gz:
+                    gz[d, k, part].wait_recv()
+                    if (d, k + 1, part) in gz:
+                        start(gz[d, k + 1, part])
 
     def rows_from(group, k):
         return 0 if group < 2 else min(k, nz - k)
@@ -316,27 +319,33 @@
     def ring(part, n, out, inn, send, recv, at):
         last = n // 2
         copies = {}
+        pieces = out.shape[2]
+        size = rows // pieces
 
         def slot(d, k):
             return (n - (last + 1 - k)) % n if d == 0 else last + 1 - k
 
         def step(d, k, h):
             begins = 1 if h == d else 2
-            value = part[slot(d, k), h * half : (h + 1) * half]
-            if k > begins:
-                copies[d, k - 1, h].wait_recv()
-                value = value + inn[d, k - 1, h].astype(F32)
-            out[d, k, h] = value.astype(BF16)
-            copies[d, k, h] = start(
-                remote(out.at[d, k, h], inn.at[d, k, h], send, recv.at[d, k - 1, h], at(1 - 2 * d))
-            )
+            for c in range(h * pieces // 2, (h + 1) * pieces // 2):
+                value = part[slot(d, k), c * size : (c + 1) * size]
+                if k > begins:
+                    copies[d, k - 1, c].wait_recv()
+                    value = value + inn[d, k - 1, c].astype(F32)
+                out[d, k, c] = value.astype(BF16)
+                copies[d, k, c] = start(
+                    remote(out.at[d, k, c], inn.at[d, k, c], send, recv.at[d, k - 1, c], at(1 - 2 * d))
+                )
 
         def owned(h):
-            copies[0, last, h].wait_recv()
-            copies[1, last, h].wait_recv()
-            value = part[0, h * half : (h + 1) * half]
-            value = value + inn[0, last, h].astype(F32) + inn[1, last, h].astype(F32)
-            return (value * inv_root).astype(BF16)
+            values = []
+            for c in range(h * pieces // 2, (h + 1) * pieces // 2):
+                copies[0, last, c].wait_recv()
+                copies[1, last, c].wait_recv()
+                value = part[0, c * size : (c + 1) * size]
+                value = value + inn[0, last, c].astype(F32) + inn[1, last, c].astype(F32)
+                values.append((value * inv_root).astype(BF16))
+            return jnp.concatenate(values, axis=0)
 
         return step, owned
 
@@ -391,10 +400,10 @@
                 back[p] = value[i * per : (i + 1) * per]
                 start(remote(back.at[p], ret.at[p], sends.at[9], rls.at[2], lang_at(p)))
 
+    send_back(1)
+    send_back(0)
     z_send(0, 4, 1)
     z_send(1, 4, 0)
-    send_back(1)
-    send_back(0)
     z_send(0, 4, 0)
     z_send(1, 4, 1)
     source_part(0)
@@ -447,11 +456,11 @@
         vmem((nz, rows, cols), BF16), vmem((nz, rows, width), F32), vmem((NY, rows, width), F32),
         vmem((3, nz, rows), F32), vmem((3, nz, nz, rows), F32), vmem((8, rows), F32), vmem((NY, 8, rows), F32),
         vmem((8, rows), F32), vmem((nz, 8, rows), F32), vmem((8, rows), F32), vmem((NY, 8, rows), F32),
-        vmem((2, kz, 2, half, width), BF16), vmem((2, kz, 2, half, width), BF16),
+        vmem((2, kz, CZ, rows // CZ, width), BF16), vmem((2, kz, CZ, rows // CZ, width), BF16),
         vmem((2, ky, 2, half, width), BF16), vmem((2, ky, 2, half, width), BF16),
         vmem((nl, per, width), BF16), vmem((nl, per, width), BF16),
-        dma((10,)), dma((4,)), dma((nz, 2)), dma((NY, 4)), dma((5,)), dma((1,)), dma((3,)),
-        dma((2, nz // 2, 2)), dma((2, NY // 2, 2)), dma((6,)),
+        dma((10,)), dma((4,)), dma((nz, CZ)), dma((NY, 4)), dma((5,)), dma((1,)), dma((3,)),
+        dma((2, nz // 2, CZ)), dma((2, NY // 2, 2)), dma((6,)),
     ]
     found = tuple(
         pl.pallas_call(

time: 52 us -> 50.7 us (0.975)
  Pallas kernels: 50.8 us -> 49.6 us
    pallas_call x1, Pallas kernels: 50 us -> 48.9 us  [per_device(): pl.pallas_call(kernel, out_shape=(pltpu.VMEM((rows, width), BF16), pltpu....]
where the time goes in v7:
time: 50.7 us; the launch traced here: 50.3 us
  Pallas kernels  49.6 us (98%)
  between operations  0.64 us (1%)
    pallas_call x1, Pallas kernels, per_device(): pl.pallas_call(kernel, out_shape=(pltpu.VMEM((rows, width), BF16), pltpu....  48.9 us

profile of v7, /device:TPU:1, one launch (start us, length us, event | category | flops | bytes accessed | tf_op | source)
XLA Modules:
  0.0 50.3 jit_solution(10384810948695875995)
XLA Ops:
  0.6 48.9 %shard_map.85 = (bf16[128,768]{1,0:T(8,128)(2,1)S(1)}, bf16[8,16,768]{2,1,0:T(8,128)(2,1)S(1)}, f32[8,128]{1,0:T(8,128)S(1)}) custom-call(s32[8]{0:T(128)} %slots_hbm.1, s32[8]{0:T(128)} %counts_hbm.1, f32[8]{0:T(128)} %weights_hbm.1, s32[1,4096]{1,0:T(1,128)} %align_hbm.1, bf16[128,768]{1,0:T(8,128)(2,1)} %x.1, bf16[8,16,768]{2,1,0:T(8,128)(2,1)} %t_hbm.1), custom_call_target="tpu_custom_call" | custom-call | tf_op jit(solution)/shard_map/pallas_call | solution.py:466
  49.5 0.8 %shard_map.86 = (bf16[128,768]{1,0:T(8,128)(2,1)}, bf16[8,16,768]{2,1,0:T(8,128)(2,1)}, f32[1]{0:T(128)}) custom-call(bf16[128,768]{1,0:T(8,128)(2,1)S(1)} %get-tuple-element.6.gsrc, bf16[8,16,768]{2,1,0:T(8,128)(2,1)S(1)} %get-tuple-element.7.gtgt, f32[8,128]{1,0:T(8,128)S(1)} %get-tuple-element.8.loss), custom_call_target="tpu_custom_call" | custom-call | tf_op jit(solution)/shard_map/pallas_call | solution.py:482

commit v8 on v7

--- a/solution.py
+++ b/solution.py
@@ -68,6 +68,17 @@
         pl.semaphore_signal(barrier, inc=1, device_id=to, device_id_type=pl.DeviceIdType.MESH)
     for copy in fetches:
         copy.start()
+    for copy in fetches[1:3]:
+        copy.wait()
+    for p in range(nl):
+        group = lang ^ p
+        slot = jnp.int32(0)
+        for s in range(nl):
+            slot = jnp.where(slots[s] == group, s, slot)
+        if p == 0:
+            ys[0, 0:per] = t[slot]
+        else:
+            staged[p] = t[slot]
     pl.semaphore_wait(barrier, len(peers))
 
     def gather_copies(first, buf, n, onward, send, recv, at):
@@ -93,17 +104,6 @@
             start(gz[1, 0, cz - 1 - i])
 
     z_begin()
-    for copy in fetches[1:3]:
-        copy.wait()
-    for p in range(nl):
-        group = lang ^ p
-        slot = jnp.int32(0)
-        for s in range(nl):
-            slot = jnp.where(slots[s] == group, s, slot)
-        if p == 0:
-            ys[0, 0:per] = t[slot]
-        else:
-            staged[p] = t[slot]
     for p in (1, 4, 5, 2, 6, 3, 7):
         start(remote(staged.at[p], ys.at[0, pl.ds(p * per, per)], sends.at[2], ra.at[p // 2], lang_at(p)))
     gy = gather_copies(ys.at[0], ys, NY, ((0, 2), (1, 3)), sends.at[1], rgy, y_at)
@@ -162,7 +162,7 @@
 
     total_pos = [jnp.zeros((1, NY * rows), F32)]
 
-    def scores(r, group):
+    def column_scores(r):
         raw = lax.dot_general(
             xs[r], all_targets(), (((1,), (1,)), ((), ())), preferred_element_type=F32
         )
@@ -171,17 +171,25 @@
         s = raw * inv_root - jnp.where(pos, MARGIN, 0.0)
         total_pos[0] += jnp.sum(jnp.where(pos & row_ok, s, 0.0), axis=0, keepdims=True)
         s = jnp.where(row_ok & col_ok, s, LOW)
+        er[r] = s
+        top = jnp.max(s, axis=0, keepdims=True)
+        e = jnp.exp(s - top)
+        ec[r] = e
+        cmax[r, 0:1] = top
+        cmax[r, 1:2] = top + jnp.log(jnp.sum(e, axis=0, keepdims=True))
+
+    def row_scores(r, group):
+        s = er[r]
         top = jnp.max(s, axis=1, keepdims=True)
         e = jnp.exp(s - top)
         er[r] = e
         row_lse = top + jnp.log(jnp.sum(e, axis=1, keepdims=True))
         rmax[r] = jnp.broadcast_to(top, (rows, rows))
         rst_out[group, r : r + 1] = jnp.broadcast_to(row_lse, (rows, rows)).T[0:1]
-        top = jnp.max(s, axis=0, keepdims=True)
-        e = jnp.exp(s - top)
-        ec[r] = e
-        cmax[r, 0:1] = top
-        cmax[r, 1:2] = top + jnp.log(jnp.sum(e, axis=0, keepdims=True))
+
+    def scores(r, group):
+        column_scores(r)
+        row_scores(r, group)
 
     def z_step(k, h):
         for i in range(h * cz // 2, (h + 1) * cz // 2):
@@ -241,7 +249,7 @@
         scores(r, 1)
     send_rows(1)
     z_step(3, 0)
-    scores(mid, 2)
+    column_scores(mid)
 
     parts = cmax[:, 1, :]
     top = jnp.max(parts, axis=0, keepdims=True)
@@ -251,6 +259,7 @@
         cst_out[q + NY : q + NY + 1] = col_part[:, q * rows : (q + 1) * rows]
     for k in range(1, NY):
         start(remote(cst_out, cst_in.at[k], sends.at[4], rcs.at[0], y_at(k)))
+    row_scores(mid, 2)
     send_rows(2)
 
     def combine(pieces):
@@ -325,17 +334,18 @@
         def slot(d, k):
             return (n - (last + 1 - k)) % n if d == 0 else last + 1 - k
 
-        def step(d, k, h):
-            begins = 1 if h == d else 2
-            for c in range(h * pieces // 2, (h + 1) * pieces // 2):
-                value = part[slot(d, k), c * size : (c + 1) * size]
-                if k > begins:
-                    copies[d, k - 1, c].wait_recv()
-                    value = value + inn[d, k - 1, c].astype(F32)
-                out[d, k, c] = value.astype(BF16)
-                copies[d, k, c] = start(
-                    remote(out.at[d, k, c], inn.at[d, k, c], send, recv.at[d, k - 1, c], at(1 - 2 * d))
-                )
+        def step(k, h):
+            for i in range(pieces // 2):
+                for d in (0, 1):
+                    c = (h if d == 0 else 1 - h) * pieces // 2 + i
+                    value = part[slot(d, k), c * size : (c + 1) * size]
+                    if k > 1 + h:
+                        copies[d, k - 1, c].wait_recv()
+                        value = value + inn[d, k - 1, c].astype(F32)
+                    out[d, k, c] = value.astype(BF16)
+                    copies[d, k, c] = start(
+                        remote(out.at[d, k, c], inn.at[d, k, c], send, recv.at[d, k - 1, c], at(1 - 2 * d))
+                    )
 
         def owned(h):
             values = []
@@ -353,30 +363,23 @@
     y_send, y_owned = ring(ptgt, NY, fy_out, fy_in, sends.at[6], rfy, y_at)
     gradient(mid)
     source_part(mid)
-    z_send(0, 1, 0)
-    z_send(1, 1, 1)
+    z_send(1, 0)
     for r in (mid + 1, mid - 1):
         gradient(r)
         source_part(r)
-    z_send(0, 2, 1)
-    z_send(1, 2, 0)
+    z_send(2, 1)
     for r in (mid + 2, mid - 2, mid + 3, mid - 3, 0):
         gradient(r)
     target_part(NY // 2)
-    y_send(0, 1, 0)
-    y_send(1, 1, 1)
-    z_send(0, 2, 0)
-    z_send(1, 2, 1)
+    y_send(1, 0)
+    z_send(2, 0)
     for q in (1, 3):
         target_part(q)
-    y_send(0, 2, 1)
-    y_send(1, 2, 0)
+    y_send(2, 1)
     for r in (mid + 2, mid - 2):
         source_part(r)
-    z_send(0, 3, 1)
-    z_send(1, 3, 0)
-    y_send(0, 2, 0)
-    y_send(1, 2, 1)
+    z_send(3, 1)
+    y_send(2, 0)
     target_part(0)
 
     own_rows = jnp.where(lane + first_row(0) < live, row_lse(0), 0.0)
@@ -385,8 +388,7 @@
     lz_out[...] = jnp.broadcast_to(own_rows + own_cols - 2.0 * pos_sum, lz_out.shape)
     for k in range(1, nz):
         start(remote(lz_out, lz_in.at[k], sends.at[7], rls.at[0], z_at(k)))
-    z_send(0, 3, 0)
-    z_send(1, 3, 1)
+    z_send(3, 0)
     for r in (mid + 3, mid - 3):
         source_part(r)
 
@@ -402,10 +404,8 @@
 
     send_back(1)
     send_back(0)
-    z_send(0, 4, 1)
-    z_send(1, 4, 0)
-    z_send(0, 4, 0)
-    z_send(1, 4, 1)
+    z_send(4, 1)
+    z_send(4, 0)
     source_part(0)
     wait_for(lz_in.at[1:nz], rls.at[0])
     ly_out[...] = functools.reduce(jnp.add, [lz_out[...]] + [lz_in[k] for k in range(1, nz)])

time: 50.7 us -> 50.4 us (level)
  no operation moved by 1% of the time
where the time goes in v8:
time: 50.4 us; the launch traced here: 50.2 us
  Pallas kernels  49.5 us (98%)
  between operations  0.64 us (1%)
    pallas_call x1, Pallas kernels, per_device(): pl.pallas_call(kernel, out_shape=(pltpu.VMEM((rows, width), BF16), pltpu....  48.8 us

profile of v8, /device:TPU:1, one launch (start us, length us, event | category | flops | bytes accessed | tf_op | source)
XLA Modules:
  0.0 50.2 jit_solution(11846498666955006554)
XLA Ops:
  0.6 48.8 %shard_map.85 = (bf16[128,768]{1,0:T(8,128)(2,1)S(1)}, bf16[8,16,768]{2,1,0:T(8,128)(2,1)S(1)}, f32[8,128]{1,0:T(8,128)S(1)}) custom-call(s32[8]{0:T(128)} %slots_hbm.1, s32[8]{0:T(128)} %counts_hbm.1, f32[8]{0:T(128)} %weights_hbm.1, s32[1,4096]{1,0:T(1,128)} %align_hbm.1, bf16[128,768]{1,0:T(8,128)(2,1)} %x.1, bf16[8,16,768]{2,1,0:T(8,128)(2,1)} %t_hbm.1), custom_call_target="tpu_custom_call" | custom-call | tf_op jit(solution)/shard_map/pallas_call | solution.py:466
  49.4 0.8 %shard_map.86 = (bf16[128,768]{1,0:T(8,128)(2,1)}, bf16[8,16,768]{2,1,0:T(8,128)(2,1)}, f32[1]{0:T(128)}) custom-call(bf16[128,768]{1,0:T(8,128)(2,1)S(1)} %get-tuple-element.6.gsrc, bf16[8,16,768]{2,1,0:T(8,128)(2,1)S(1)} %get-tuple-element.7.gtgt, f32[8,128]{1,0:T(8,128)S(1)} %get-tuple-element.8.loss), custom_call_target="tpu_custom_call" | custom-call | tf_op jit(solution)/shard_map/pallas_call | solution.py:482

commit v9 on v8

--- a/solution.py
+++ b/solution.py
@@ -457,10 +457,10 @@
         vmem((3, nz, rows), F32), vmem((3, nz, nz, rows), F32), vmem((8, rows), F32), vmem((NY, 8, rows), F32),
         vmem((8, rows), F32), vmem((nz, 8, rows), F32), vmem((8, rows), F32), vmem((NY, 8, rows), F32),
         vmem((2, kz, CZ, rows // CZ, width), BF16), vmem((2, kz, CZ, rows // CZ, width), BF16),
-        vmem((2, ky, 2, half, width), BF16), vmem((2, ky, 2, half, width), BF16),
+        vmem((2, ky, 4, half // 2, width), BF16), vmem((2, ky, 4, half // 2, width), BF16),
         vmem((nl, per, width), BF16), vmem((nl, per, width), BF16),
         dma((10,)), dma((4,)), dma((nz, CZ)), dma((NY, 4)), dma((5,)), dma((1,)), dma((3,)),
-        dma((2, nz // 2, CZ)), dma((2, NY // 2, 2)), dma((6,)),
+        dma((2, nz // 2, CZ)), dma((2, NY // 2, 4)), dma((6,)),
     ]
     found = tuple(
         pl.pallas_call(

time: 50.4 us -> 50.5 us (level)
  no operation moved by 1% of the time
where the time goes in v9:
time: 50.5 us; the launch traced here: 50.2 us
  Pallas kernels  49.6 us (98%)
  between operations  0.64 us (1%)
    pallas_call x1, Pallas kernels, per_device(): pl.pallas_call(kernel, out_shape=(pltpu.VMEM((rows, width), BF16), pltpu....  48.8 us

profile of v9, /device:TPU:1, one launch (start us, length us, event | category | flops | bytes accessed | tf_op | source)
XLA Modules:
  0.0 50.2 jit_solution(5175864205796897650)
XLA Ops:
  0.6 48.8 %shard_map.85 = (bf16[128,768]{1,0:T(8,128)(2,1)S(1)}, bf16[8,16,768]{2,1,0:T(8,128)(2,1)S(1)}, f32[8,128]{1,0:T(8,128)S(1)}) custom-call(s32[8]{0:T(128)} %slots_hbm.1, s32[8]{0:T(128)} %counts_hbm.1, f32[8]{0:T(128)} %weights_hbm.1, s32[1,4096]{1,0:T(1,128)} %align_hbm.1, bf16[128,768]{1,0:T(8,128)(2,1)} %x.1, bf16[8,16,768]{2,1,0:T(8,128)(2,1)} %t_hbm.1), custom_call_target="tpu_custom_call" | custom-call | tf_op jit(solution)/shard_map/pallas_call | solution.py:466
  49.4 0.8 %shard_map.86 = (bf16[128,768]{1,0:T(8,128)(2,1)}, bf16[8,16,768]{2,1,0:T(8,128)(2,1)}, f32[1]{0:T(128)}) custom-call(bf16[128,768]{1,0:T(8,128)(2,1)S(1)} %get-tuple-element.6.gsrc, bf16[8,16,768]{2,1,0:T(8,128)(2,1)S(1)} %get-tuple-element.7.gtgt, f32[8,128]{1,0:T(8,128)S(1)} %get-tuple-element.8.loss), custom_call_target="tpu_custom_call" | custom-call | tf_op jit(solution)/shard_map/pallas_call | solution.py:482

commit v10 on v8

--- a/solution.py
+++ b/solution.py
@@ -227,9 +227,9 @@
     y_begin(3)
     z_step(0, 1)
     y_begin(2)
+    z_step(1, 0)
     y_on(0, 0)
     y_on(1, 1)
-    z_step(1, 0)
     y_on(1, 3)
     y_on(0, 2)
     z_step(1, 1)

time: 50.4 us -> 50.4 us (level)
  no operation moved by 1% of the time
where the time goes in v10:
time: 50.4 us; the launch traced here: 50.2 us
  Pallas kernels  49.5 us (98%)
  between operations  0.64 us (1%)
    pallas_call x1, Pallas kernels, per_device(): pl.pallas_call(kernel, out_shape=(pltpu.VMEM((rows, width), BF16), pltpu....  48.8 us

profile of v10, /device:TPU:1, one launch (start us, length us, event | category | flops | bytes accessed | tf_op | source)
XLA Modules:
  0.0 50.2 jit_solution(8937156516585854456)
XLA Ops:
  0.6 48.8 %shard_map.85 = (bf16[128,768]{1,0:T(8,128)(2,1)S(1)}, bf16[8,16,768]{2,1,0:T(8,128)(2,1)S(1)}, f32[8,128]{1,0:T(8,128)S(1)}) custom-call(s32[8]{0:T(128)} %slots_hbm.1, s32[8]{0:T(128)} %counts_hbm.1, f32[8]{0:T(128)} %weights_hbm.1, s32[1,4096]{1,0:T(1,128)} %align_hbm.1, bf16[128,768]{1,0:T(8,128)(2,1)} %x.1, bf16[8,16,768]{2,1,0:T(8,128)(2,1)} %t_hbm.1), custom_call_target="tpu_custom_call" | custom-call | tf_op jit(solution)/shard_map/pallas_call | solution.py:466
  49.4 0.8 %shard_map.86 = (bf16[128,768]{1,0:T(8,128)(2,1)}, bf16[8,16,768]{2,1,0:T(8,128)(2,1)}, f32[1]{0:T(128)}) custom-call(bf16[128,768]{1,0:T(8,128)(2,1)S(1)} %get-tuple-element.6.gsrc, bf16[8,16,768]{2,1,0:T(8,128)(2,1)S(1)} %get-tuple-element.7.gtgt, f32[8,128]{1,0:T(8,128)S(1)} %get-tuple-element.8.loss), custom_call_target="tpu_custom_call" | custom-call | tf_op jit(solution)/shard_map/pallas_call | solution.py:482
